TPU v7x, 32 devices: a whole 2x2x4 slice. The times are simulated.
32 devices in a mesh: dp: 16 (over z, x, core), tensor: 2 (over y).
Axes of the slice: x: 2, y: 2, z: 4, core: 2. Of those that a mesh axis runs over, the one named last changes fastest.
Arguments:
- hidden: bfloat16 [2048, 4096], P('dp', 'tensor'), may hold values from -6 to 6
- gain: bfloat16 [4096], P('tensor'), may hold values from 0.5 to 1.5
- w_query: bfloat16 [4096, 4096], P('dp', 'tensor'), may hold values from -0.09375 to 0.09375
- w_key: bfloat16 [4096, 1024], P('dp', 'tensor'), may hold values from -0.09375 to 0.09375
- w_value: bfloat16 [4096, 1024], P('dp', 'tensor'), may hold values from -0.09375 to 0.09375
- cotangent: bfloat16 [4096, 4096], P('dp', 'tensor'), may hold values from -6 to 6
- seq_length: int32 [16, 4], replicated, may hold values from 16 to 64, as said below
- home_offset: int32 [16, 4], replicated, may hold values from 0 to 112, as said below
- dest_shard: int32 [16, 4], replicated, may hold values from 0 to 15, as said below
- dest_offset: int32 [16, 4], replicated, may hold values from 0 to 192, as said below
Outputs:
- attention_output: bfloat16 [4096, 4096], P('dp', 'tensor')
- grad_hidden: bfloat16 [2048, 4096], P('dp', 'tensor')
- grad_value_weight: float32 [4096, 1024], P('dp', 'tensor')
Inputs may be any that keep to these rules, and one draw needn't show every extreme that they name: `seq_length`: the 4 sequences of a shard fill its 128 rows exactly; every length is at least 16 and at most 64, and some sequence has length 64. `home_offset`: the sequences of a shard lie back to back from row 0 in the order of c. `dest_shard`: sequence c of shard h goes to shard (h + e) mod 16, e one of -1, 1, 8 and 9; every shard sends exactly one sequence to each of these 4 shards. `dest_offset`: the sequences that arrive at a shard lie back to back from row 0 of its 256 rows, in the order e = -1, 1, 8, 9; at some shard they fill all 256 rows.
All inputs are finite; a program needn't handle non-finite values.
Results may differ from a plain program's by a relative error of at most 0.02.
Values may be sent and summed in bfloat16 or wider, within the bound.
A program may use at most 128 MiB of HBM per device.

v0:
```python
import jax
import jax.numpy as jnp
from jax import lax
from jax.sharding import PartitionSpec as P

D = 4096
HEAD = 128
TOK_DEV = 128
MAXLEN = 64
CAP = 256


EPSILON = 1e-05
ROPE_BASE = 500000.0


def passed_along(value, axis, by):
    size = lax.axis_size(axis)
    return lax.ppermute(value, axis, [(i, (i + by) % size) for i in range(size)])


def rope_tables(position):
    half_head = HEAD // 2
    exponent = jnp.arange(half_head, dtype=jnp.float32) * (2.0 / HEAD)
    inverse = jnp.power(jnp.float32(ROPE_BASE), -exponent)
    angles = position.astype(jnp.float32)[:, None] * inverse[None, :]
    return (jnp.cos(angles)[:, None, :], jnp.sin(angles)[:, None, :])


def rotate(values, cosine, sine_part):
    half_head = values.shape[-1] // 2
    lower_half = values[..., :half_head]
    upper_half = values[..., half_head:]
    return jnp.concatenate(
        [
            lower_half * cosine - upper_half * sine_part,
            upper_half * cosine + lower_half * sine_part,
        ],
        -1,
    )


def unrotate(values, cosine, sine_part):
    half_head = values.shape[-1] // 2
    lower_half = values[..., :half_head]
    upper_half = values[..., half_head:]
    return jnp.concatenate(
        [
            lower_half * cosine + upper_half * sine_part,
            upper_half * cosine - lower_half * sine_part,
        ],
        -1,
    )


def attention_block(normed, w_query, w_key, w_value, cotangent, segment, position, occupied):
    row_count = normed.shape[0]
    kv_heads = w_key.shape[1] // HEAD
    q_heads = w_query.shape[1] // HEAD
    group_size = q_heads // kv_heads
    cosine, sine_part = rope_tables(position)
    query_rows = jnp.dot(normed, w_query, preferred_element_type=jnp.float32).reshape(
        row_count, q_heads, HEAD
    )
    key_rows = jnp.dot(normed, w_key, preferred_element_type=jnp.float32).reshape(
        row_count, kv_heads, HEAD
    )
    value_rows = (
        jnp.dot(normed, w_value, preferred_element_type=jnp.float32)
        .astype(jnp.bfloat16)
        .reshape(row_count, kv_heads, HEAD)
    )
    query_rows = (
        rotate(query_rows, cosine, sine_part)
        .astype(jnp.bfloat16)
        .reshape(row_count, kv_heads, group_size, HEAD)
    )
    key_rows = rotate(key_rows, cosine, sine_part).astype(jnp.bfloat16)
    factor = HEAD ** (-0.5)
    scores = (
        jnp.einsum("qhgd,khd->hgqk", query_rows, key_rows, preferred_element_type=jnp.float32)
        * factor
    )
    allowed = (segment[:, None] == segment[None, :]) & (position[None, :] <= position[:, None])
    scores = jnp.where(allowed[None, None], scores, jnp.float32(-1e30))
    row_max = jnp.max(scores, -1, keepdims=True)
    exp_terms = jnp.exp(scores - row_max)
    attn_prob = exp_terms / jnp.sum(exp_terms, -1, keepdims=True)
    prob_low = attn_prob.astype(jnp.bfloat16)
    mixed_rows = jnp.einsum(
        "hgqk,khd->qhgd", prob_low, value_rows, preferred_element_type=jnp.float32
    )
    attn_out = jnp.where(
        occupied[:, None], mixed_rows.reshape(row_count, q_heads * HEAD), jnp.float32(0.0)
    ).astype(jnp.bfloat16)
    grad_out = jnp.where(occupied[:, None], cotangent, jnp.zeros((), jnp.bfloat16)).reshape(
        row_count, kv_heads, group_size, HEAD
    )
    grad_value = jnp.einsum(
        "hgqk,qhgd->khd", prob_low, grad_out, preferred_element_type=jnp.float32
    ).astype(jnp.bfloat16)
    grad_probs = jnp.einsum(
        "qhgd,khd->hgqk", grad_out, value_rows, preferred_element_type=jnp.float32
    )
    centre = jnp.sum(grad_probs * attn_prob, -1, keepdims=True)
    grad_scores = (attn_prob * (grad_probs - centre) * factor).astype(jnp.bfloat16)
    grad_query = jnp.einsum(
        "hgqk,khd->qhgd", grad_scores, key_rows, preferred_element_type=jnp.float32
    ).reshape(row_count, q_heads, HEAD)
    grad_key = jnp.einsum(
        "hgqk,qhgd->khd", grad_scores, query_rows, preferred_element_type=jnp.float32
    )
    grad_query = (
        unrotate(grad_query, cosine, sine_part)
        .astype(jnp.bfloat16)
        .reshape(row_count, q_heads * HEAD)
    )
    grad_key = (
        unrotate(grad_key, cosine, sine_part)
        .astype(jnp.bfloat16)
        .reshape(row_count, kv_heads * HEAD)
    )
    return (attn_out, grad_query, grad_key, grad_value.reshape(row_count, kv_heads * HEAD))


def cut_blocks(matrix, starts, lengths):
    within = jnp.arange(MAXLEN, dtype=jnp.int32)
    picks = jnp.minimum(starts[:, None] + within[None, :], matrix.shape[0] - 1)
    in_seq = within[None, :] < lengths[:, None]
    return jnp.where(in_seq[:, :, None], matrix[picks], jnp.zeros((), matrix.dtype))


def on_device(
    hidden,
    gain,
    w_query,
    w_key,
    w_value,
    cotangent,
    seq_length,
    home_offset,
    dest_shard,
    dest_offset,
):
    shards = lax.axis_size("dp")
    my_shard = lax.axis_index("dp")
    width_here = hidden.shape[1]
    shift_list = [-1, 1, shards // 2, shards // 2 + 1]
    stride_array = jnp.array(shift_list, dtype=jnp.int32)
    stride_mod = jnp.array([stride % shards for stride in shift_list], dtype=jnp.int32)
    slot_count = len(shift_list)
    slot_index = jnp.arange(slot_count, dtype=jnp.int32)[:, None]
    wq_full, wk_full, wv_full = (
        lax.all_gather(w_query, "dp", axis=0, tiled=True),
        lax.all_gather(w_key, "dp", axis=0, tiled=True),
        lax.all_gather(w_value, "dp", axis=0, tiled=True),
    )
    own_len = seq_length[my_shard]
    own_off = home_offset[my_shard]
    own_move = (dest_shard[my_shard] - my_shard + shards) % shards
    chosen = (own_move[None, :] == stride_mod[:, None]).astype(jnp.int32)
    outgoing = cut_blocks(
        hidden, jnp.sum(chosen * own_off[None, :], 1), jnp.sum(chosen * own_len[None, :], 1)
    )
    buffers = jnp.zeros((shards, MAXLEN, width_here), hidden.dtype)
    for number, stride in enumerate(shift_list):
        buffers = lax.dynamic_update_slice_in_dim(
            buffers, outgoing[number][None], (my_shard + stride + shards) % shards, 0
        )
    received = lax.all_to_all(buffers, "dp", split_axis=0, concat_axis=0, tiled=True)
    arrived = jnp.stack(
        [
            lax.dynamic_index_in_dim(
                received, (my_shard - stride + shards) % shards, 0, keepdims=False
            )
            for stride in shift_list
        ]
    )
    sources = (my_shard - stride_array + shards) % shards
    source_move = (dest_shard[sources] - sources[:, None] + shards) % shards
    matches = (source_move == stride_mod[:, None]).astype(jnp.int32)
    in_len = jnp.sum(matches * seq_length[sources], 1)
    in_start = jnp.sum(matches * dest_offset[sources], 1)
    dest_slot = jnp.arange(CAP, dtype=jnp.int32)
    member = (
        (dest_slot[None, :] >= in_start[:, None])
        & (dest_slot[None, :] < (in_start + in_len)[:, None])
    ).astype(jnp.int32)
    occupied = jnp.sum(member, 0) > 0
    segment = jnp.where(occupied, jnp.sum(member * slot_index, 0), -1)
    position = jnp.sum(member * (dest_slot[None, :] - in_start[:, None]), 0)
    fetch_rows = jnp.sum(member * (slot_index * MAXLEN + dest_slot[None, :] - in_start[:, None]), 0)
    local_rows = jnp.where(
        occupied[:, None], arrived.reshape(-1, width_here)[fetch_rows], jnp.zeros((), hidden.dtype)
    )
    full_rows, gain_full = (
        lax.all_gather(local_rows, "tensor", axis=1, tiled=True),
        lax.all_gather(gain, "tensor", axis=0, tiled=True),
    )
    values = full_rows.astype(jnp.float32)
    inverse_rms = lax.rsqrt(jnp.mean(values * values, 1, keepdims=True) + EPSILON)
    normed = (values * inverse_rms * gain_full.astype(jnp.float32)).astype(jnp.bfloat16)
    attn_out, grad_query, grad_key, grad_value = attention_block(
        normed, wq_full, wk_full, wv_full, cotangent, segment, position, occupied
    )
    partial_value = jnp.einsum("rc,dc->rd", grad_query, wq_full, preferred_element_type=jnp.float32)
    partial_value = partial_value + jnp.einsum(
        "rc,dc->rd", grad_key, wk_full, preferred_element_type=jnp.float32
    )
    partial_value = partial_value + jnp.einsum(
        "rc,dc->rd", grad_value, wv_full, preferred_element_type=jnp.float32
    )
    grad_value_weight = lax.psum_scatter(
        jnp.einsum("rd,rc->dc", normed, grad_value, preferred_element_type=jnp.float32),
        "dp",
        scatter_dimension=0,
        tiled=True,
    )
    slot_of_seq = jnp.sum(chosen * slot_index, 0)
    home_slot = jnp.arange(TOK_DEV, dtype=jnp.int32)
    belong = (
        (home_slot[None, :] >= own_off[:, None])
        & (home_slot[None, :] < (own_off + own_len)[:, None])
    ).astype(jnp.int32)
    gather_back = jnp.sum(
        belong * (slot_of_seq[:, None] * MAXLEN + home_slot[None, :] - own_off[:, None]), 0
    )
    gain_here = gain.astype(jnp.float32)
    summed = lax.psum_scatter(
        partial_value.astype(jnp.bfloat16), "tensor", scatter_dimension=1, tiled=True
    ).astype(jnp.float32)
    weighted = summed * gain_here
    local_vals = local_rows.astype(jnp.float32)
    row_dot = lax.psum(jnp.sum(weighted * local_vals, 1), "tensor")
    grad_rows = (
        inverse_rms * weighted - local_vals * inverse_rms**3 * row_dot[:, None] / D
    ).astype(jnp.bfloat16)
    sending = cut_blocks(grad_rows, in_start, in_len)
    returned = jnp.stack(
        [passed_along(sending[number], "dp", -stride) for number, stride in enumerate(shift_list)]
    )
    grad_hidden = returned.reshape(-1, width_here)[gather_back]
    return (attn_out, grad_hidden, grad_value_weight)


def solution(mesh):
    return jax.shard_map(
        on_device,
        mesh=mesh,
        in_specs=(
            P("dp", "tensor"),
            P("tensor"),
            P("dp", "tensor"),
            P("dp", "tensor"),
            P("dp", "tensor"),
            P("dp", "tensor"),
            P(),
            P(),
            P(),
            P(),
        ),
        out_specs=(P("dp", "tensor"), P("dp", "tensor"), P("dp", "tensor")),
        check_vma=False,
    )
```

profile of v0, /device:TPU:26, one launch (start us, length us, event | category | flops | bytes accessed | tf_op | source)
XLA Modules:
  0.0 616.6 jit_solution(17831803022805781490)
XLA Ops:
  7.2 0.8 copy.82
  8.0 0.9 fusion.40
  8.9 0.9 fusion.45
  9.8 0.8 copy.80
  10.5 0.9 fusion.41
  11.4 0.9 fusion.37
  12.4 0.7 compare_select_fusion.4
  13.0 0.8 copy.81
  14.4 0.6 gather_fusion.2
  15.5 0.9 select_reduce_fusion.4
  16.5 1.4 gather_fusion.3
  18.1 2.5 broadcast_in_dim.62
  20.5 0.7 slice_dynamic-update-slice_fusion.3
  21.3 0.7 slice_dynamic-update-slice_fusion.2
  22.0 0.7 slice_dynamic-update-slice_fusion.1
  22.7 0.7 slice_dynamic-update-slice_fusion
  23.4 6.0 all-to-all-start
  29.7 91.1 %all-to-all-done = bf16[16,64,2048]{2,1,0:T(8,128)(2,1)} async-done(((bf16[16,64,2048]{2,1,0:T(8,128)(2,1)}), bf16[16,64,2048]{2,1,0:T(8,128)(2,1)}, u32[]{:S(2)}, u32[]{:S(2)}) %all-to-all-start) | async-done | bytes 4194336 | tf_op jit(solution)/shard_map/all_to_all | solution.py:170
  120.8 1.3 constant_dynamic-slice_fusion.3
  122.2 1.4 gather_fusion.4
  123.6 1.1 broadcast_select_fusion.1
  124.8 0.7 all-gather.7.cloned.1.call-update
  125.5 0.7 all-gather.9.cloned.1.call-update
  126.9 4.5 all_gather.16
  132.1 26.9 %all-gather.5.cloned.1.call-done = bf16[256,4096]{1,0:T(8,128)(2,1)} async-done(((bf16[256,2048]{1,0:T(8,128)(2,1)}), bf16[256,4096]{1,0:T(8,128)(2,1)}) %all-gather.5.cloned.1.call-update) | async-done | bytes 2097168 | tf_op jit(solution)/shard_map/all_gather | solution.py:197
  159.0 2.1 fusion.3
  161.1 48.2 %all-gather.7.cloned.1.call-done = bf16[4096,512]{1,0:T(8,128)(2,1)} async-done(((bf16[256,512]{1,0:T(8,128)(2,1)}), bf16[4096,512]{1,0:T(8,128)(2,1)}) %all-gather.7.cloned.1.call-update) | async-done | bytes 4194320 | tf_op jit(solution)/shard_map/all_gather | solution.py:156
  209.3 4.1 convolution_convert_fusion
  213.5 47.1 %all-gather.9.cloned.1.call-done = bf16[4096,512]{1,0:T(8,128)(2,1)} async-done(((bf16[256,512]{1,0:T(8,128)(2,1)}), bf16[4096,512]{1,0:T(8,128)(2,1)}) %all-gather.9.cloned.1.call-update) | async-done | bytes 4194320 | tf_op jit(solution)/shard_map/all_gather | solution.py:155
  260.6 4.1 fusion.58
  265.4 122.1 %all-gather.11.cloned.1.call-done = bf16[4096,2048]{1,0:T(8,128)(2,1)} async-done(((bf16[256,2048]{1,0:T(8,128)(2,1)}), bf16[4096,2048]{1,0:T(8,128)(2,1)}) %all-gather.11.cloned.1.call-update) | async-done | bytes 16777232 | tf_op jit(solution)/shard_map/all_gather | solution.py:154
  387.5 8.8 %convolution_bitcast_fusion = f32[32,8,16,128]{3,1,2,0:T(8,128)S(1)} fusion(bf16[4096,2048]{1,0:T(8,128)(2,1)} %all-gather.11.cloned.1.call-done, bf16[256,4096]{1,0:T(8,128)(2,1)} %all-gather.5.cloned.1.call-done, f32[4096]{0:T(1024)S(1)} %convert_element_type.70, f32[256]{0:T(256)S(1)} %get-tuple-element.39), kind=kOutput, calls=%fused_computation.45 | convolution fusion | flops 4299161600 | bytes 20988928 | tf_op jit(solution)/shard_map/dot_general | solution.py:62
  396.7 0.8 subtract_convert_fusion.1
  397.7 1.3 copy.86
  399.1 5.2 fusion.63
  404.3 3.7 fusion.27
  408.0 1.5 copy.89
  409.5 3.2 broadcast_select_fusion
  412.7 1.7 copy.124
  414.4 3.0 fusion.22
  417.4 2.6 fusion.32
  420.0 8.3 %fusion.21 = f32[256,4,128]{2,0,1:T(8,128)S(1)} fusion(f32[4,256,256,4]{2,1,3,0:T(8,128)} %fusion.32, bf16[256,4,4,64]{3,0,2,1:T(8,128)(2,1)} %bitcast.134, bf16[256,4,4,64]{3,0,2,1:T(8,128)(2,1)} %bitcast.132, f32[4,4,256,256]{2,3,1,0:T(8,128)} %get-tuple-element.43, f32[4,4,256]{2,1,0:T(4,128)S(1)} %get-tuple-element.42), kind=kOutput, calls=%fused_computation.46 | convolution fusion | flops 277876992 | bytes 9977856 | tf_op jit(solution)/shard_map/hgqk,qhgd->khd/dot_general | solution.py:110
  428.4 8.7 %fusion.20 = f32[4,128,4,256]{3,1,2,0:T(8,128)} fusion(f32[4,256,256,4]{2,1,3,0:T(8,128)} %fusion.32, bf16[256,4,64]{2,0,1:T(8,128)(2,1)S(1)} %copy-done.7, bf16[256,4,64]{2,0,1:T(8,128)(2,1)S(1)} %copy-done.5, f32[4,4,256,256]{2,3,1,0:T(8,128)} %get-tuple-element.43, f32[4,4,256]{2,1,0:T(4,128)S(1)} %get-tuple-element.42), kind=kOutput, calls=%fused_computation.44 | convolution fusion | flops 276304128 | bytes 10764288 | tf_op jit(solution)/shard_map/hgqk,khd->qhgd/dot_general | solution.py:107
  437.1 2.7 fusion.61
  440.4 3.8 copy.123
  444.2 2.4 copy.122
  446.6 2.8 add_convert_fusion
  449.4 0.6 pad_maximum_fusion.2
  450.0 10.5 %fusion.23 = f32[256,4096]{1,0:T(8,128)} fusion(bf16[4096,2048]{1,0:T(8,128)(2,1)} %all-gather.11.cloned.1.call-done, bf16[32,8,16,128]{3,2,1,0:T(8,128)(2,1)S(1)} %bitcast.127), kind=kOutput, calls=%fused_computation.50 | convolution fusion | flops 4294967296 | bytes 22020096 | tf_op jit(solution)/shard_map/rc,dc->rd/dot_general | solution.py:206
  460.5 4.9 convolution_add_fusion.1
  465.4 2.7 fusion.2
  468.2 6.2 %fusion.55 = f32[4096,512]{1,0:T(8,128)} fusion(bf16[256,512]{0,1:T(8,128)(2,1)S(1)} %bitcast.129, bf16[256,4096]{1,0:T(8,128)(2,1)} %all-gather.5.cloned.1.call-done, f32[4096]{0:T(1024)S(1)} %convert_element_type.70, f32[256]{0:T(256)S(1)} %get-tuple-element.39), kind=kOutput, calls=%fused_computation.156 | convolution fusion | flops 1077936128 | bytes 10765312 | tf_op jit(solution)/shard_map/rd,rc->dc/dot_general | solution.py:214
  474.7 26.5 %reduce-scatter.3.cloned.1.call-done = bf16[256,2048]{1,0:T(8,128)(2,1)} async-done(((bf16[256,4096]{1,0:T(8,128)(2,1)}), bf16[256,2048]{1,0:T(8,128)(2,1)}) %reduce-scatter.3.cloned.1.call-update) | async-done | bytes 1048592 | tf_op jit(solution)/shard_map/reduce_scatter | solution.py:229
  501.2 1.7 fusion.14
  503.0 4.9 psum.7
  507.9 2.1 fusion.13
  510.0 1.4 gather_fusion.5
  511.7 1.7 collective-permute-start.3
  513.4 2.4 collective-permute-start.2
  515.8 4.5 collective-permute-done
  520.3 14.0 %collective-permute-done.3 = bf16[64,2048]{1,0:T(8,128)(2,1)S(1)} collective-permute-done((bf16[64,2048]{1,0:T(8,128)(2,1)S(1)}, bf16[64,2048]{1,0:T(8,128)(2,1)S(1)}, u32[]{:S(2)}, u32[]{:S(2)}) %collective-permute-start.3) | collective-permute-done | bytes 262176 | tf_op jit(solution)/shard_map/ppermute | solution.py:19
  534.3 9.0 %collective-permute-done.2 = bf16[64,2048]{1,0:T(8,128)(2,1)S(1)} collective-permute-done((bf16[64,2048]{1,0:T(8,128)(2,1)S(1)}, bf16[64,2048]{1,0:T(8,128)(2,1)S(1)}, u32[]{:S(2)}, u32[]{:S(2)}) %collective-permute-start.2) | collective-permute-done | bytes 262176 | tf_op jit(solution)/shard_map/ppermute | solution.py:19
  543.5 1.7 gather_fusion.6
  545.2 64.6 %reduce-scatter.5.cloned.1.call-done = f32[256,512]{1,0:T(8,128)} async-done(((f32[4096,512]{1,0:T(8,128)}), f32[256,512]{1,0:T(8,128)}) %reduce-scatter.5.cloned.1.call-update) | async-done | bytes 524304 | tf_op jit(solution)/shard_map/reduce_scatter | solution.py:213
  (73 shorter events, 5.9 us)
Async XLA Ops:
  7.2 9.4 %copy-start = (bf16[128,2048]{1,0:T(8,128)(2,1)S(1)}, bf16[128,2048]{1,0:T(8,128)(2,1)}, u32[]{:S(2)}) copy-start(bf16[128,2048]{1,0:T(8,128)(2,1)} %param.12) | copy-start | bytes 1572868
  23.4 97.4 %all-to-all-start = ((bf16[16,64,2048]{2,1,0:T(8,128)(2,1)}), bf16[16,64,2048]{2,1,0:T(8,128)(2,1)}, u32[]{:S(2)}, u32[]{:S(2)}) async-start(bf16[16,64,2048]{2,1,0:T(8,128)(2,1)} %slice_dynamic-update-slice_fusion), calls=%async_computation | async-start | bytes 8388608 | tf_op jit(solution)/shard_map/all_to_all | solution.py:170
  29.5 129.5 %all-gather.5.cloned.1.call-start = ((), (), s32[]{:S(2)}) async-start(), calls=%async_computation.3 | async-start | bytes 3145728 | tf_op jit(solution)/shard_map/all_gather | solution.py:197
  123.6 3.3 copy-start.8
  124.7 84.6 %all-gather.7.cloned.1.call-start = ((), (), s32[]{:S(2)}) async-start(), calls=%async_computation.4 | async-start | bytes 4456448 | tf_op jit(solution)/shard_map/all_gather | solution.py:156
  125.5 135.1 %all-gather.9.cloned.1.call-start = ((), (), s32[]{:S(2)}) async-start(), calls=%async_computation.5 | async-start | bytes 4456448 | tf_op jit(solution)/shard_map/all_gather | solution.py:155
  126.2 261.3 %all-gather.11.cloned.1.call-start = ((), (), s32[]{:S(2)}) async-start(), calls=%async_computation.6 | async-start | bytes 17825792 | tf_op jit(solution)/shard_map/all_gather | solution.py:154
  126.8 374.4 %reduce-scatter.3.cloned.1.call-start = ((), (), s32[]{:S(2)}) async-start(), calls=%async_computation.7 | async-start | bytes 3145728 | tf_op jit(solution)/shard_map/reduce_scatter | solution.py:229
  265.4 133.7 %copy-start.4 = (bf16[256,4,64]{2,0,1:T(8,128)(2,1)}, bf16[256,4,64]{2,0,1:T(8,128)(2,1)S(1)}, u32[]{:S(2)}) copy-start(bf16[256,4,64]{2,0,1:T(8,128)(2,1)S(1)} %get-tuple-element.26) | copy-start | bytes 393220
  265.4 133.7 %copy-start.6 = (bf16[256,4,64]{2,0,1:T(8,128)(2,1)}, bf16[256,4,64]{2,0,1:T(8,128)(2,1)S(1)}, u32[]{:S(2)}) copy-start(bf16[256,4,64]{2,0,1:T(8,128)(2,1)S(1)} %get-tuple-element.27) | copy-start | bytes 393220
  397.7 6.5 %copy-start.3 = (bf16[256,16,64]{2,0,1:T(8,128)(2,1)}, bf16[256,16,64]{2,0,1:T(8,128)(2,1)S(1)}, u32[]{:S(2)}) copy-start(bf16[256,16,64]{2,0,1:T(8,128)(2,1)S(1)} %copy.85) | copy-start | bytes 1572868
  420.0 8.4 %copy-start.5 = (bf16[256,4,64]{2,0,1:T(8,128)(2,1)S(1)}, bf16[256,4,64]{2,0,1:T(8,128)(2,1)}, u32[]{:S(2)}) copy-start(bf16[256,4,64]{2,0,1:T(8,128)(2,1)} %copy-done.4) | copy-start | bytes 393220
  420.0 8.4 %copy-start.7 = (bf16[256,4,64]{2,0,1:T(8,128)(2,1)S(1)}, bf16[256,4,64]{2,0,1:T(8,128)(2,1)}, u32[]{:S(2)}) copy-start(bf16[256,4,64]{2,0,1:T(8,128)(2,1)} %copy-done.6) | copy-start | bytes 393220
  460.5 4.9 copy-start.2
  468.1 141.6 %reduce-scatter.5.cloned.1.call-start = ((), (), s32[]{:S(2)}) async-start(), calls=%async_computation.8 | async-start | bytes 8912896 | tf_op jit(solution)/shard_map/reduce_scatter | solution.py:213
  511.4 98.4 %copy-start.1 = (bf16[128,2048]{1,0:T(8,128)(2,1)S(1)}, bf16[128,2048]{1,0:T(8,128)(2,1)}, u32[]{:S(2)}) copy-start(bf16[128,2048]{1,0:T(8,128)(2,1)} %param.12) | copy-start | bytes 1572868
  511.6 8.7 %collective-permute-start = (bf16[64,2048]{1,0:T(8,128)(2,1)S(1)}, bf16[64,2048]{1,0:T(8,128)(2,1)S(1)}, u32[]{:S(2)}, u32[]{:S(2)}) collective-permute-start(bf16[64,2048]{1,0:T(8,128)(2,1)S(1)} %get-tuple-element.28), channel_id=1, source_target_pairs={{0,2},{2,4},{4,6},{6,8},{8,10},{10,12},{12,14},{14,16},{16,18},{18... | collective-permute-start | bytes 786440 | tf_op jit(solution)/shard_map/ppermute | solution.py:19
  511.7 22.6 %collective-permute-start.3 = (bf16[64,2048]{1,0:T(8,128)(2,1)S(1)}, bf16[64,2048]{1,0:T(8,128)(2,1)S(1)}, u32[]{:S(2)}, u32[]{:S(2)}) collective-permute-start(bf16[64,2048]{1,0:T(8,128)(2,1)S(1)} %get-tuple-element.29), channel_id=1, source_target_pairs={{0,14},{2,16},{4,18},{6,20},{8,22},{10,24},{12,26},{14,28},{16,30}... | collective-permute-start | bytes 786440 | tf_op jit(solution)/shard_map/ppermute | solution.py:19
  513.4 29.9 %collective-permute-start.2 = (bf16[64,2048]{1,0:T(8,128)(2,1)S(1)}, bf16[64,2048]{1,0:T(8,128)(2,1)S(1)}, u32[]{:S(2)}, u32[]{:S(2)}) collective-permute-start(bf16[64,2048]{1,0:T(8,128)(2,1)S(1)} %get-tuple-element.30), channel_id=1, source_target_pairs={{0,16},{2,18},{4,20},{6,22},{8,24},{10,26},{12,28},{14,30},{16,0},... | collective-permute-start | bytes 786440 | tf_op jit(solution)/shard_map/ppermute | solution.py:19
  515.8 27.5 %collective-permute-start.1 = (bf16[64,2048]{1,0:T(8,128)(2,1)S(1)}, bf16[64,2048]{1,0:T(8,128)(2,1)S(1)}, u32[]{:S(2)}, u32[]{:S(2)}) collective-permute-start(bf16[64,2048]{1,0:T(8,128)(2,1)S(1)} %get-tuple-element.31), channel_id=1, source_target_pairs={{0,30},{2,0},{4,2},{6,4},{8,6},{10,8},{12,10},{14,12},{16,14},{18,... | collective-permute-start | bytes 786440 | tf_op jit(solution)/shard_map/ppermute | solution.py:19
Sparse Core Ops, SparseCore 0:
  124.9 34.0 all-gather.4
  161.1 48.1 all-gather.6
  211.5 49.0 all-gather.8
  262.6 124.8 all-gather.10
  468.3 32.9 reduce-scatter.2
  506.3 103.4 reduce-scatter.4
where the time goes:
time: 620 us; the launch traced here: 617 us
  waiting for transfers between devices  456 us (74%)
  matrix products  73 us (12%)
  local copies, waits for them, and re-layouts  33.3 us (5%)
  other arithmetic  19.9 us (3%)
  between operations  14.6 us (2%)
  starting transfers between devices  10.4 us (2%)
  blocking collectives  9.46 us (2%)
    all_gather x1, waiting for transfers between devices, on_device(): lax.all_gather(w_query, 'dp', axis=0, tiled=True)  122 us
    all_to_all x1, waiting for transfers between devices, on_device(): lax.all_to_all(buffers, 'dp', split_axis=0, concat_axis=0, tiled=True)  91.1 us
    reduce_scatter x1, waiting for transfers between devices, on_device(): lax.psum_scatter(jnp.einsum('rd,rc->dc', normed, grad_value, preferred_el...  64.6 us
    all_gather x1, waiting for transfers between devices, on_device(): lax.all_gather(w_value, 'dp', axis=0, tiled=True)  48.2 us
    all_gather x1, waiting for transfers between devices, on_device(): lax.all_gather(w_key, 'dp', axis=0, tiled=True)  47.1 us
    ppermute x4, waiting for transfers between devices, passed_along(): lax.ppermute(value, axis, [(i, (i + by) % size) for i in range(size)])  27.5 us
    all_gather x1, waiting for transfers between devices, on_device(): lax.all_gather(local_rows, 'tensor', axis=1, tiled=True)  26.9 us
    reduce_scatter x1, waiting for transfers between devices, on_device(): lax.psum_scatter(partial_value.astype(jnp.bfloat16), 'tensor', scatter_di...  26.5 us
  transfers between devices with their start and end apart: 11, of which 10 were waited for; matrix products, arithmetic and copies ran while one was open for 4% of the time, Pallas kernels for 0%

commit v1 on v0

v1 whole, which is shorter than its diff:
```python
import jax
import jax.numpy as jnp
from jax import lax
from jax.sharding import PartitionSpec as P

D = 4096
HEAD = 128
TOK_DEV = 128
MAXLEN = 64
CAP = 256


EPSILON = 1e-05
ROPE_BASE = 500000.0


def passed_along(value, axis, by):
    size = lax.axis_size(axis)
    return lax.ppermute(value, axis, [(i, (i + by) % size) for i in range(size)])


def rope_tables(position):
    half_head = HEAD // 2
    exponent = jnp.arange(half_head, dtype=jnp.float32) * (2.0 / HEAD)
    inverse = jnp.power(jnp.float32(ROPE_BASE), -exponent)
    angles = position.astype(jnp.float32)[:, None] * inverse[None, :]
    return (jnp.cos(angles)[:, None, :], jnp.sin(angles)[:, None, :])


def rotate(values, cosine, sine_part):
    half_head = values.shape[-1] // 2
    lower_half = values[..., :half_head]
    upper_half = values[..., half_head:]
    return jnp.concatenate(
        [
            lower_half * cosine - upper_half * sine_part,
            upper_half * cosine + lower_half * sine_part,
        ],
        -1,
    )


def attention_block(normed, w_query, w_key, w_value, cotangent, segment, position):
    row_count = normed.shape[0]
    kv_heads = w_key.shape[1] // HEAD
    q_heads = w_query.shape[1] // HEAD
    group_size = q_heads // kv_heads
    cosine, sine_part = rope_tables(position)
    query_rows = jnp.dot(normed, w_query, preferred_element_type=jnp.float32).reshape(
        row_count, q_heads, HEAD
    )
    key_rows = jnp.dot(normed, w_key, preferred_element_type=jnp.float32).reshape(
        row_count, kv_heads, HEAD
    )
    value_rows = (
        jnp.dot(normed, w_value, preferred_element_type=jnp.float32)
        .astype(jnp.bfloat16)
        .reshape(row_count, kv_heads, HEAD)
    )
    query_rows = (
        rotate(query_rows, cosine, sine_part)
        .astype(jnp.bfloat16)
        .reshape(row_count, kv_heads, group_size, HEAD)
    )
    key_rows = rotate(key_rows, cosine, sine_part).astype(jnp.bfloat16)
    factor = HEAD ** (-0.5)
    scores = (
        jnp.einsum("qhgd,khd->hgqk", query_rows, key_rows, preferred_element_type=jnp.float32)
        * factor
    )
    allowed = (segment[:, None] == segment[None, :]) & (position[None, :] <= position[:, None])
    scores = jnp.where(allowed[None, None], scores, jnp.float32(-1e30))
    row_max = jnp.max(scores, -1, keepdims=True)
    exp_terms = jnp.exp(scores - row_max)
    attn_prob = exp_terms / jnp.sum(exp_terms, -1, keepdims=True)
    prob_low = attn_prob.astype(jnp.bfloat16)
    attn_out = (
        jnp.einsum("hgqk,khd->qhgd", prob_low, value_rows, preferred_element_type=jnp.float32)
        .reshape(row_count, q_heads * HEAD)
        .astype(jnp.bfloat16)
    )
    grad_out = cotangent.reshape(row_count, kv_heads, group_size, HEAD)
    grad_value = jnp.einsum(
        "hgqk,qhgd->khd", prob_low, grad_out, preferred_element_type=jnp.float32
    ).astype(jnp.bfloat16)
    grad_probs = jnp.einsum(
        "qhgd,khd->hgqk", grad_out, value_rows, preferred_element_type=jnp.float32
    )
    centre = jnp.sum(grad_probs * attn_prob, -1, keepdims=True)
    grad_scores = (attn_prob * (grad_probs - centre) * factor).astype(jnp.bfloat16)
    grad_query = jnp.einsum(
        "hgqk,khd->qhgd", grad_scores, key_rows, preferred_element_type=jnp.float32
    ).reshape(row_count, q_heads, HEAD)
    grad_key = jnp.einsum(
        "hgqk,qhgd->khd", grad_scores, query_rows, preferred_element_type=jnp.float32
    )
    grad_query = (
        rotate(grad_query, cosine, -sine_part)
        .astype(jnp.bfloat16)
        .reshape(row_count, q_heads * HEAD)
    )
    grad_key = (
        rotate(grad_key, cosine, -sine_part)
        .astype(jnp.bfloat16)
        .reshape(row_count, kv_heads * HEAD)
    )
    return (attn_out, grad_query, grad_key, grad_value.reshape(row_count, kv_heads * HEAD))


def pick_rows(selection, matrix):
    return jnp.dot(
        selection.astype(jnp.bfloat16), matrix, preferred_element_type=jnp.float32
    ).astype(jnp.bfloat16)


def on_device(
    hidden,
    gain,
    w_query,
    w_key,
    w_value,
    cotangent,
    seq_length,
    home_offset,
    dest_shard,
    dest_offset,
):
    shards = lax.axis_size("dp")
    my_shard = lax.axis_index("dp")
    width_here = hidden.shape[1]
    shift_list = [-1, 1, shards // 2, shards // 2 + 1]
    stride_array = jnp.array(shift_list, dtype=jnp.int32)
    stride_mod = jnp.array([stride % shards for stride in shift_list], dtype=jnp.int32)
    wq_full, wk_full, wv_full = (
        lax.all_gather(w_query, "dp", axis=0, tiled=True),
        lax.all_gather(w_key, "dp", axis=0, tiled=True),
        lax.all_gather(w_value, "dp", axis=0, tiled=True),
    )
    own_len = seq_length[my_shard]
    own_off = home_offset[my_shard]
    own_move = (dest_shard[my_shard] - my_shard + shards) % shards
    chosen = (own_move[None, :] == stride_mod[:, None]).astype(jnp.int32)
    slot_len = jnp.sum(chosen * own_len[None, :], 1)
    slot_off = jnp.sum(chosen * own_off[None, :], 1)
    sources = (my_shard - stride_array + shards) % shards
    source_move = (dest_shard[sources] - sources[:, None] + shards) % shards
    matches = (source_move == stride_mod[:, None]).astype(jnp.int32)
    in_len = jnp.sum(matches * seq_length[sources], 1)
    in_start = jnp.sum(matches * dest_offset[sources], 1)
    within = jnp.arange(MAXLEN, dtype=jnp.int32)[None, :, None]

    def cuts(starts, lengths, rows):
        row = jnp.arange(rows, dtype=jnp.int32)[None, None, :]
        return (within < lengths[:, None, None]) & (row == starts[:, None, None] + within)

    home_cut = cuts(slot_off, slot_len, TOK_DEV).reshape(-1, TOK_DEV)
    dest_cut = cuts(in_start, in_len, CAP).reshape(-1, CAP)
    cot_blocks = pick_rows(dest_cut, cotangent).reshape(-1, MAXLEN, width_here)
    cot_home = jnp.concatenate(
        [passed_along(cot_blocks[i], "dp", -stride) for i, stride in enumerate(shift_list)], 0
    )
    cot_home = pick_rows(home_cut.T, cot_home)
    home_slot = jnp.arange(TOK_DEV, dtype=jnp.int32)
    belong = (
        (home_slot[None, :] >= own_off[:, None])
        & (home_slot[None, :] < (own_off + own_len)[:, None])
    ).astype(jnp.int32)
    start_of = jnp.sum(belong * own_off[:, None], 0)
    position = home_slot - start_of

    rows_full, gain_full = (
        lax.all_gather(hidden, "tensor", axis=1, tiled=True),
        lax.all_gather(gain, "tensor", axis=0, tiled=True),
    )
    values = rows_full.astype(jnp.float32)
    inverse_rms = lax.rsqrt(jnp.mean(values * values, 1, keepdims=True) + EPSILON)
    normed = (values * inverse_rms * gain_full.astype(jnp.float32)).astype(jnp.bfloat16)
    normed_columns = lax.all_to_all(normed, "dp", split_axis=1, concat_axis=0, tiled=True)
    attn_out, grad_query, grad_key, grad_value = attention_block(
        normed, wq_full, wk_full, wv_full, cot_home, start_of, position
    )
    out_blocks = pick_rows(home_cut, attn_out).reshape(-1, MAXLEN, width_here)
    out_dest = jnp.concatenate(
        [passed_along(out_blocks[i], "dp", stride) for i, stride in enumerate(shift_list)], 0
    )
    attention_output = pick_rows(dest_cut.T, out_dest)
    value_all = lax.all_gather(grad_value, "dp", axis=0, tiled=True)
    grad_value_weight = jnp.einsum(
        "rd,rc->dc", normed_columns, value_all, preferred_element_type=jnp.float32
    )
    partial_value = jnp.einsum("rc,dc->rd", grad_query, wq_full, preferred_element_type=jnp.float32)
    partial_value = partial_value + jnp.einsum(
        "rc,dc->rd", grad_key, wk_full, preferred_element_type=jnp.float32
    )
    partial_value = partial_value + jnp.einsum(
        "rc,dc->rd", grad_value, wv_full, preferred_element_type=jnp.float32
    )
    gain_here = gain.astype(jnp.float32)
    summed = lax.psum_scatter(
        partial_value.astype(jnp.bfloat16), "tensor", scatter_dimension=1, tiled=True
    ).astype(jnp.float32)
    weighted = summed * gain_here
    local_vals = hidden.astype(jnp.float32)
    row_dot = lax.psum(jnp.sum(weighted * local_vals, 1), "tensor")
    grad_hidden = (
        inverse_rms * weighted - local_vals * inverse_rms**3 * row_dot[:, None] / D
    ).astype(jnp.bfloat16)
    return (attention_output, grad_hidden, grad_value_weight)


def solution(mesh):
    return jax.shard_map(
        on_device,
        mesh=mesh,
        in_specs=(
            P("dp", "tensor"),
            P("tensor"),
            P("dp", "tensor"),
            P("dp", "tensor"),
            P("dp", "tensor"),
            P("dp", "tensor"),
            P(),
            P(),
            P(),
            P(),
        ),
        out_specs=(P("dp", "tensor"), P("dp", "tensor"), P("dp", "tensor")),
        check_vma=False,
    )
```

time: 620 us -> 401 us (0.65)
  waiting for transfers between devices: 456 us -> 270 us
  local copies, waits for them, and re-layouts: 33.3 us -> 13.6 us
  matrix products: 73 us -> 58.9 us
  other arithmetic: 19.9 us -> 11.4 us
  starting transfers between devices: 10.4 us -> 17.9 us
    reduce_scatter x1 -> x0, waiting for transfers between devices: 64.6 us -> none  [on_device(): lax.psum_scatter(jnp.einsum('rd,rc->dc', normed, grad_value, preferred_el...]
    all_to_all x1, waiting for transfers between devices: 91.1 us -> 29.7 us  [on_device(): lax.all_to_all(normed, 'dp', split_axis=1, concat_axis=0, tiled=True)]
    all_gather x1 -> x2, waiting for transfers between devices: 26.9 us -> 0.02 us  [the longest x1 0.02 us: on_device(): lax.all_gather(hidden, 'tensor', axis=1, tiled=True)]
    reduce_scatter x1, waiting for transfers between devices: 26.5 us -> 0.01 us  [on_device(): lax.psum_scatter(partial_value.astype(jnp.bfloat16), 'tensor', scatter_di...]
    all_gather x1, waiting for transfers between devices: 47.1 us -> 32.9 us  [on_device(): lax.all_gather(w_key, 'dp', axis=0, tiled=True)]
    ppermute x4 -> x8, starting transfers between devices: 4.16 us -> 10.7 us  [passed_along(): lax.ppermute(value, axis, [(i, (i + by) % size) for i in range(size)])]
    ppermute x4 -> x8, waiting for transfers between devices: 27.5 us -> 33.6 us  [passed_along(): lax.ppermute(value, axis, [(i, (i + by) % size) for i in range(size)])]
  transfers between devices with their start and end apart: 11 -> 15, of which waited for: 10 -> 8; matrix products, arithmetic and copies ran while one was open for 4% -> 7% of each run, Pallas kernels for 0% -> 0%
where the time goes in v1:
time: 401 us; the launch traced here: 395 us
  waiting for transfers between devices  270 us (67%)
  matrix products  58.9 us (15%)
  starting transfers between devices  17.9 us (4%)
  between operations  14.6 us (4%)
  local copies, waits for them, and re-layouts  13.6 us (3%)
  other arithmetic  11.4 us (3%)
  blocking collectives  9.35 us (2%)
    all_gather x1, waiting for transfers between devices, on_device(): lax.all_gather(w_query, 'dp', axis=0, tiled=True)  123 us
    all_gather x1, waiting for transfers between devices, on_device(): lax.all_gather(w_value, 'dp', axis=0, tiled=True)  47.9 us
    ppermute x8, waiting for transfers between devices, passed_along(): lax.ppermute(value, axis, [(i, (i + by) % size) for i in range(size)])  33.6 us
    all_gather x1, waiting for transfers between devices, on_device(): lax.all_gather(w_key, 'dp', axis=0, tiled=True)  32.9 us
    all_to_all x1, waiting for transfers between devices, on_device(): lax.all_to_all(normed, 'dp', split_axis=1, concat_axis=0, tiled=True)  29.7 us
    dot_general x1, matrix products, on_device(): jnp.einsum('rc,dc->rd', grad_query, wq_full, preferred_element_type=jnp.f...  13 us
    ppermute x8, starting transfers between devices, passed_along(): lax.ppermute(value, axis, [(i, (i + by) % size) for i in range(size)])  10.7 us
    dot_general x1, matrix products, attention_block(): jnp.dot(normed, w_query, preferred_element_type=jnp.float32)  8.46 us
  transfers between devices with their start and end apart: 15, of which 8 were waited for; matrix products, arithmetic and copies ran while one was open for 7% of the time, Pallas kernels for 0%

profile of v1, /device:TPU:26, one launch (start us, length us, event | category | flops | bytes accessed | tf_op | source)
XLA Modules:
  0.0 395.3 jit_solution(4907628192272359307)
XLA Ops:
  7.3 2.1 copy.105
  9.5 0.7 all-gather.10.cloned.1.call-update
  10.2 0.7 all-gather.8.cloned.1.call-update
  11.0 0.5 all-gather.12.cloned.1.call-update
  11.7 0.6 gather_fusion
  12.3 0.6 gather_fusion.1
  13.0 0.6 gather_fusion.2
  13.5 0.2 select_reduce_fusion.2
  14.1 0.5 copy-done.20
  14.6 0.5 convolution_convert_fusion.1
  15.2 1.7 collective-permute-start.5
  17.0 0.3 collective-permute-start.6
  17.3 1.7 collective-permute-start.7
  19.2 0.2 fusion.69
  20.2 4.4 %all_gather.19 = bf16[4096]{0:T(1024)(128)(2,1)S(1)} all-gather(bf16[2048]{0:T(1024)(128)(2,1)S(1)} %copy-done.11), channel_id=1, replica_groups=mesh['dp'=16,'tensor'=2] {'tensor'}, dimensions={0}, use_global_device_ids=true | all-gather | bytes 12288 | tf_op jit(solution)/shard_map/all_gather | solution.py:173
  24.6 0.3 fusion.63
  25.0 12.9 %collective-permute-done.6 = bf16[64,2048]{1,0:T(8,128)(2,1)S(1)} collective-permute-done((bf16[64,2048]{1,0:T(8,128)(2,1)S(1)}, bf16[64,2048]{1,0:T(8,128)(2,1)S(1)}, u32[]{:S(2)}, u32[]{:S(2)}) %collective-permute-start.6) | collective-permute-done | bytes 262176 | tf_op jit(solution)/shard_map/ppermute | solution.py:19
  37.8 5.6 %collective-permute-done.7 = bf16[64,2048]{1,0:T(8,128)(2,1)} collective-permute-done((bf16[64,2048]{1,0:T(8,128)(2,1)S(1)}, bf16[64,2048]{1,0:T(8,128)(2,1)}, u32[]{:S(2)}, u32[]{:S(2)}) %collective-permute-start.7) | collective-permute-done | bytes 262176 | tf_op jit(solution)/shard_map/ppermute | solution.py:19
  43.4 1.4 convolution_convert_fusion.3
  44.9 0.3 copy.147
  45.2 1.8 fusion.3
  47.0 0.6 multiply_multiply_fusion
  47.5 2.5 fusion.5
  50.0 32.9 %all-gather.10.cloned.1.call-done = bf16[4096,512]{1,0:T(8,128)(2,1)} async-done(((bf16[256,512]{1,0:T(8,128)(2,1)}), bf16[4096,512]{1,0:T(8,128)(2,1)}) %all-gather.10.cloned.1.call-update) | async-done | bytes 4194320 | tf_op jit(solution)/shard_map/all_gather | solution.py:136
  82.9 3.2 fusion.91
  86.3 47.9 %all-gather.8.cloned.1.call-done = bf16[4096,512]{1,0:T(8,128)(2,1)} async-done(((bf16[256,512]{1,0:T(8,128)(2,1)}), bf16[4096,512]{1,0:T(8,128)(2,1)}) %all-gather.8.cloned.1.call-update) | async-done | bytes 4194320 | tf_op jit(solution)/shard_map/all_gather | solution.py:137
  134.2 3.3 convolution_convert_fusion.5
  137.5 0.2 fusion.89
  137.8 0.3 convolution_bitcast_fusion
  138.1 123.0 %all-gather.12.cloned.1.call-done = bf16[4096,2048]{1,0:T(8,128)(2,1)} async-done(((bf16[256,2048]{1,0:T(8,128)(2,1)}), bf16[4096,2048]{1,0:T(8,128)(2,1)}) %all-gather.12.cloned.1.call-update) | async-done | bytes 16777232 | tf_op jit(solution)/shard_map/all_gather | solution.py:135
  261.1 8.5 %convolution_bitcast_fusion.1 = f32[16,8,16,128]{3,1,2,0:T(8,128)S(1)} fusion(bf16[128,4096]{0,1:T(8,128)(2,1)} %fusion.5, bf16[4096,2048]{1,0:T(8,128)(2,1)} %all-gather.12.cloned.1.call-done), kind=kOutput, calls=%fused_computation.26 | convolution fusion | flops 2147483648 | bytes 18874368 | tf_op jit(solution)/shard_map/dot_general | solution.py:49
  269.8 0.5 subtract_convert_fusion.1
  270.3 0.9 copy.108
  271.2 0.9 copy.109
  272.2 2.9 fusion.90
  275.1 2.1 fusion.14
  277.2 2.6 convolution_bitcast_fusion.2
  279.9 3.2 fusion.38
  283.4 2.1 fusion.86
  285.6 0.5 copy.145
  286.1 1.5 copy.146
  287.6 0.3 subtract_convert_fusion
  287.9 0.3 pad_maximum_fusion.1
  288.2 13.0 %fusion.40 = f32[128,4096]{1,0:T(8,128)} fusion(bf16[4096,2048]{1,0:T(8,128)(2,1)} %all-gather.12.cloned.1.call-done, bf16[16,8,16,128]{3,2,1,0:T(8,128)(2,1)S(1)} %bitcast.94), kind=kOutput, calls=%fused_computation.62 | convolution fusion | flops 2147483648 | bytes 19398656 | tf_op jit(solution)/shard_map/rc,dc->rd/dot_general | solution.py:191
  301.2 4.4 %convolution_add_fusion.1 = f32[128,4096]{1,0:T(8,128)S(1)} fusion(f32[128,4096]{1,0:T(8,128)} %fusion.40, bf16[128,512]{0,1:T(8,128)(2,1)S(1)} %bitcast.101, bf16[4096,512]{1,0:T(8,128)(2,1)} %all-gather.10.cloned.1.call-done), kind=kOutput, calls=%fused_computation.6 | convolution fusion | flops 537395200 | bytes 8519680 | tf_op jit(solution)/shard_map/rc,dc->rd/dot_general | solution.py:192
  305.6 4.7 %fusion.2 = bf16[128,4096]{1,0:T(8,128)(2,1)} fusion(f32[128,4096]{1,0:T(8,128)S(1)} %convolution_add_fusion.1, bf16[128,512]{0,1:T(8,128)(2,1)S(1)} %bitcast.99, bf16[4096,512]{1,0:T(8,128)(2,1)} %all-gather.8.cloned.1.call-done), kind=kOutput, calls=%fused_computation.7 | convolution fusion | flops 537919488 | bytes 7471104 | tf_op jit(solution)/shard_map/rc,dc->rd/dot_general | solution.py:195
  310.3 0.5 all-gather.14.cloned.1.call-update
  310.8 7.0 %all-to-all-start = ((bf16[128,16,256]{0,2,1:T(8,128)(2,1)}), bf16[128,16,256]{0,2,1:T(8,128)(2,1)S(1)}, u32[]{:S(2)}, u32[]{:S(2)}) async-start(bf16[128,16,256]{0,2,1:T(8,128)(2,1)} %bitcast.22), calls=%async_computation.1 | async-start | bytes 2097152 | tf_op jit(solution)/shard_map/all_to_all | solution.py:178
  317.8 1.9 convolution_convert_fusion.4
  319.8 1.1 convolution_convert_fusion
  320.9 0.9 fusion.88
  321.8 0.3 collective-permute-start
  322.1 0.2 collective-permute-start.1
  322.3 0.5 collective-permute-start.2
  322.8 5.8 %collective-permute-start.3 = (bf16[64,2048]{1,0:T(8,128)(2,1)S(1)}, bf16[64,2048]{1,0:T(8,128)(2,1)}, u32[]{:S(2)}, u32[]{:S(2)}) collective-permute-start(bf16[64,2048]{1,0:T(8,128)(2,1)S(1)} %get-tuple-element.20), channel_id=1, source_target_pairs={{0,18},{2,20},{4,22},{6,24},{8,26},{10,28},{12,30},{14,0},{16,2},{... | collective-permute-start | bytes 786440 | tf_op jit(solution)/shard_map/ppermute | solution.py:19
  328.7 29.7 %all-to-all-done = bf16[128,16,256]{0,2,1:T(8,128)(2,1)S(1)} async-done(((bf16[128,16,256]{0,2,1:T(8,128)(2,1)}), bf16[128,16,256]{0,2,1:T(8,128)(2,1)S(1)}, u32[]{:S(2)}, u32[]{:S(2)}) %all-to-all-start) | async-done | bytes 1048608 | tf_op jit(solution)/shard_map/all_to_all | solution.py:178
  358.4 0.5 copy.124
  359.0 4.8 %collective-permute-done.2 = bf16[64,2048]{1,0:T(8,128)(2,1)} collective-permute-done((bf16[64,2048]{1,0:T(8,128)(2,1)}, bf16[64,2048]{1,0:T(8,128)(2,1)}, u32[]{:S(2)}, u32[]{:S(2)}) %collective-permute-start.2) | collective-permute-done | bytes 262176 | tf_op jit(solution)/shard_map/ppermute | solution.py:19
  363.8 10.3 %collective-permute-done.3 = bf16[64,2048]{1,0:T(8,128)(2,1)} collective-permute-done((bf16[64,2048]{1,0:T(8,128)(2,1)S(1)}, bf16[64,2048]{1,0:T(8,128)(2,1)}, u32[]{:S(2)}, u32[]{:S(2)}) %collective-permute-start.3) | collective-permute-done | bytes 262176 | tf_op jit(solution)/shard_map/ppermute | solution.py:19
  374.0 2.7 convolution_convert_fusion.2
  376.8 1.3 fusion.19
  378.1 4.9 %psum.7 = f32[128]{0:T(128)S(1)} all-reduce(f32[128]{0:T(128)S(1)} %fusion.19), channel_id=1, replica_groups=mesh['dp'=16,'tensor'=2] {'tensor'}, use_global_device_ids=true, to_apply=%region_11.12 | all-reduce | flops 128 | bytes 1024 | tf_op jit(solution)/shard_map/psum | solution.py:204
  383.0 2.3 fusion.18
  385.3 3.1 fusion.92
  (93 shorter events, 2.8 us)
Async XLA Ops:
  7.2 7.4 %copy-start = (bf16[256,2048]{1,0:T(8,128)(2,1)S(1)}, bf16[256,2048]{1,0:T(8,128)(2,1)}, u32[]{:S(2)}) copy-start(bf16[256,2048]{1,0:T(8,128)(2,1)} %param.17) | copy-start | bytes 3145732
  7.2 4.5 %copy-start.22 = (s32[4]{0:T(128)S(1)}, s32[4]{0:T(128)}, u32[]{:S(2)}) copy-start(s32[4]{0:T(128)} %constant.68) | copy-start | bytes 52
  7.2 6.3 %copy-start.17 = (s32[4]{0:T(128)S(1)}, s32[4]{0:T(128)}, u32[]{:S(2)}) copy-start(s32[4]{0:T(128)} %constant.67.clone) | copy-start | bytes 52
  7.2 4.3 %copy-start.13 = (s32[16,4]{0,1:T(4,128)S(1)}, s32[16,4]{0,1:T(4,128)}, u32[]{:S(2)}) copy-start(s32[16,4]{0,1:T(4,128)} %param.20) | copy-start | bytes 772
  7.2 4.4 %copy-start.14 = (s32[16,4]{0,1:T(4,128)S(1)}, s32[16,4]{0,1:T(4,128)}, u32[]{:S(2)}) copy-start(s32[16,4]{0,1:T(4,128)} %param.18) | copy-start | bytes 772
  7.2 5.6 %copy-start.15 = (s32[16,4]{0,1:T(4,128)S(1)}, s32[16,4]{0,1:T(4,128)}, u32[]{:S(2)}) copy-start(s32[16,4]{0,1:T(4,128)} %param.21) | copy-start | bytes 772
  7.2 37.9 %all-gather.6.cloned.1.call-start = ((), (), s32[]{:S(2)}) async-start(), calls=%async_computation.2 | async-start | bytes 1572864 | tf_op jit(solution)/shard_map/all_gather | solution.py:172
  9.4 73.5 %all-gather.10.cloned.1.call-start = ((), (), s32[]{:S(2)}) async-start(), calls=%async_computation.4 | async-start | bytes 4456448 | tf_op jit(solution)/shard_map/all_gather | solution.py:136
  10.2 124.0 %all-gather.8.cloned.1.call-start = ((), (), s32[]{:S(2)}) async-start(), calls=%async_computation.3 | async-start | bytes 4456448 | tf_op jit(solution)/shard_map/all_gather | solution.py:137
  10.9 250.2 %all-gather.12.cloned.1.call-start = ((), (), s32[]{:S(2)}) async-start(), calls=%async_computation.5 | async-start | bytes 17825792 | tf_op jit(solution)/shard_map/all_gather | solution.py:135
  11.5 365.3 %reduce-scatter.2.cloned.1.call-start = ((), (), s32[]{:S(2)}) async-start(), calls=%async_computation.6 | async-start | bytes 1572864 | tf_op jit(solution)/shard_map/reduce_scatter | solution.py:199
  14.1 0.5 copy-start.20
  14.6 4.7 %copy-start.16 = (s32[16,4]{0,1:T(4,128)S(1)}, s32[16,4]{0,1:T(4,128)}, u32[]{:S(2)}) copy-start(s32[16,4]{0,1:T(4,128)} %param.19) | copy-start | bytes 772
  14.6 5.6 %copy-start.11 = (bf16[2048]{0:T(1024)(128)(2,1)S(1)}, bf16[2048]{0:T(1024)(128)(2,1)}, u32[]{:S(2)}) copy-start(bf16[2048]{0:T(1024)(128)(2,1)} %param.13) | copy-start | bytes 12292
  15.2 9.8 %collective-permute-start.4 = (bf16[64,2048]{1,0:T(8,128)(2,1)S(1)}, bf16[64,2048]{1,0:T(8,128)(2,1)S(1)}, u32[]{:S(2)}, u32[]{:S(2)}) collective-permute-start(bf16[64,2048]{1,0:T(8,128)(2,1)S(1)} %get-tuple-element.15), channel_id=1, source_target_pairs={{0,2},{2,4},{4,6},{6,8},{8,10},{10,12},{12,14},{14,16},{16,18},{18... | collective-permute-start | bytes 786440 | tf_op jit(solution)/shard_map/ppermute | solution.py:19
  15.2 9.7 %collective-permute-start.5 = (bf16[64,2048]{1,0:T(8,128)(2,1)S(1)}, bf16[64,2048]{1,0:T(8,128)(2,1)S(1)}, u32[]{:S(2)}, u32[]{:S(2)}) collective-permute-start(bf16[64,2048]{1,0:T(8,128)(2,1)S(1)} %get-tuple-element.18), channel_id=1, source_target_pairs={{0,30},{2,0},{4,2},{6,4},{8,6},{10,8},{12,10},{14,12},{16,14},{18,... | collective-permute-start | bytes 786440 | tf_op jit(solution)/shard_map/ppermute | solution.py:19
  17.0 20.9 %collective-permute-start.6 = (bf16[64,2048]{1,0:T(8,128)(2,1)S(1)}, bf16[64,2048]{1,0:T(8,128)(2,1)S(1)}, u32[]{:S(2)}, u32[]{:S(2)}) collective-permute-start(bf16[64,2048]{1,0:T(8,128)(2,1)S(1)} %get-tuple-element.17), channel_id=1, source_target_pairs={{0,16},{2,18},{4,20},{6,22},{8,24},{10,26},{12,28},{14,30},{16,0},... | collective-permute-start | bytes 786440 | tf_op jit(solution)/shard_map/ppermute | solution.py:19
  17.3 26.1 %collective-permute-start.7 = (bf16[64,2048]{1,0:T(8,128)(2,1)S(1)}, bf16[64,2048]{1,0:T(8,128)(2,1)}, u32[]{:S(2)}, u32[]{:S(2)}) collective-permute-start(bf16[64,2048]{1,0:T(8,128)(2,1)S(1)} %get-tuple-element.16), channel_id=1, source_target_pairs={{0,14},{2,16},{4,18},{6,20},{8,22},{10,24},{12,26},{14,28},{16,30}... | collective-permute-start | bytes 786440 | tf_op jit(solution)/shard_map/ppermute | solution.py:19
  20.0 255.1 %copy-start.12 = (pred[128,128]{0,1:T(8,128)(4,1)}, pred[128,128]{0,1:T(8,128)(4,1)S(1)}, u32[]{:S(2)}) copy-start(pred[128,128]{0,1:T(8,128)(4,1)S(1)} %compare_and_fusion) | copy-start | bytes 49156
  20.2 24.9 %copy-start.19 = (pred[256]{0:T(512)(128)(4,1)}, pred[256]{0:T(512)(128)(4,1)S(1)}, u32[]{:S(2)}) copy-start(pred[256]{0:T(512)(128)(4,1)S(1)} %lt.96) | copy-start | bytes 772
  137.5 132.1 %copy-start.4 = (bf16[128,4,128]{2,1,0:T(4,128)(2,1)}, bf16[128,4,128]{2,1,0:T(4,128)(2,1)S(1)}, u32[]{:S(2)}) copy-start(bf16[128,4,128]{2,1,0:T(4,128)(2,1)S(1)} %reshape.339) | copy-start | bytes 393220
  137.8 137.3 %copy-start.8 = (bf16[128,4,64]{2,0,1:T(8,128)(2,1)}, bf16[128,4,64]{2,0,1:T(8,128)(2,1)S(1)}, u32[]{:S(2)}) copy-start(bf16[128,4,64]{2,0,1:T(8,128)(2,1)S(1)} %get-tuple-element.24) | copy-start | bytes 196612
  137.8 142.1 %copy-start.6 = (bf16[128,4,64]{2,0,1:T(8,128)(2,1)}, bf16[128,4,64]{2,0,1:T(8,128)(2,1)S(1)}, u32[]{:S(2)}) copy-start(bf16[128,4,64]{2,0,1:T(8,128)(2,1)S(1)} %get-tuple-element.23) | copy-start | bytes 196612
  275.1 4.8 %copy-start.23 = (f32[4,4,128]{2,1,0:T(4,128)}, f32[4,4,128]{2,1,0:T(4,128)S(1)}, u32[]{:S(2)}) copy-start(f32[4,4,128]{2,1,0:T(4,128)S(1)} %get-tuple-element.36) | copy-start | bytes 24580
  277.2 28.4 %copy-start.2 = (bf16[4,128,128]{2,1,0:T(8,128)(2,1)}, bf16[4,128,128]{2,1,0:T(8,128)(2,1)S(1)}, u32[]{:S(2)}) copy-start(bf16[4,128,128]{2,1,0:T(8,128)(2,1)S(1)} %fusion.14) | copy-start | bytes 393220
  277.2 2.7 copy-start.9
  310.2 7.6 %copy-start.3 = (bf16[128,16,64]{2,0,1:T(8,128)(2,1)S(1)}, bf16[128,16,64]{2,0,1:T(8,128)(2,1)}, u32[]{:S(2)}) copy-start(bf16[128,16,64]{2,0,1:T(8,128)(2,1)} %copy.108) | copy-start | bytes 786436
  310.2 7.6 %copy-start.5 = (bf16[128,4,128]{2,1,0:T(4,128)(2,1)S(1)}, bf16[128,4,128]{2,1,0:T(4,128)(2,1)}, u32[]{:S(2)}) copy-start(bf16[128,4,128]{2,1,0:T(4,128)(2,1)} %copy-done.4) | copy-start | bytes 393220
  310.2 7.6 %copy-start.7 = (bf16[128,4,64]{2,0,1:T(8,128)(2,1)S(1)}, bf16[128,4,64]{2,0,1:T(8,128)(2,1)}, u32[]{:S(2)}) copy-start(bf16[128,4,64]{2,0,1:T(8,128)(2,1)} %copy-done.6) | copy-start | bytes 196612
  310.2 7.6 %copy-start.10 = (bf16[128,4,64]{2,0,1:T(8,128)(2,1)S(1)}, bf16[128,4,64]{2,0,1:T(8,128)(2,1)}, u32[]{:S(2)}) copy-start(bf16[128,4,64]{2,0,1:T(8,128)(2,1)} %copy-done.8) | copy-start | bytes 196612
  310.3 75.1 %all-gather.14.cloned.1.call-start = ((), (), s32[]{:S(2)}) async-start(), calls=%async_computation.7 | async-start | bytes 2228224 | tf_op jit(solution)/shard_map/all_gather | solution.py:187
  310.8 47.6 %all-to-all-start = ((bf16[128,16,256]{0,2,1:T(8,128)(2,1)}), bf16[128,16,256]{0,2,1:T(8,128)(2,1)S(1)}, u32[]{:S(2)}, u32[]{:S(2)}) async-start(bf16[128,16,256]{0,2,1:T(8,128)(2,1)} %bitcast.22), calls=%async_computation.1 | async-start | bytes 2097152 | tf_op jit(solution)/shard_map/all_to_all | solution.py:178
  320.9 53.2 %copy-start.21 = (pred[256]{0:T(512)(128)(4,1)S(1)}, pred[256]{0:T(512)(128)(4,1)}, u32[]{:S(2)}) copy-start(pred[256]{0:T(512)(128)(4,1)} %copy-done.20) | copy-start | bytes 772
  321.8 37.1 %collective-permute-start = (bf16[64,2048]{1,0:T(8,128)(2,1)}, bf16[64,2048]{1,0:T(8,128)(2,1)}, u32[]{:S(2)}, u32[]{:S(2)}) collective-permute-start(bf16[64,2048]{1,0:T(8,128)(2,1)} %get-tuple-element.19), channel_id=1, source_target_pairs={{0,30},{2,0},{4,2},{6,4},{8,6},{10,8},{12,10},{14,12},{16,14},{18,... | collective-permute-start | bytes 786440 | tf_op jit(solution)/shard_map/ppermute | solution.py:19
  322.1 36.8 %collective-permute-start.1 = (bf16[64,2048]{1,0:T(8,128)(2,1)}, bf16[64,2048]{1,0:T(8,128)(2,1)}, u32[]{:S(2)}, u32[]{:S(2)}) collective-permute-start(bf16[64,2048]{1,0:T(8,128)(2,1)} %get-tuple-element.22), channel_id=1, source_target_pairs={{0,2},{2,4},{4,6},{6,8},{8,10},{10,12},{12,14},{14,16},{16,18},{18... | collective-permute-start | bytes 786440 | tf_op jit(solution)/shard_map/ppermute | solution.py:19
  322.3 41.4 %collective-permute-start.2 = (bf16[64,2048]{1,0:T(8,128)(2,1)}, bf16[64,2048]{1,0:T(8,128)(2,1)}, u32[]{:S(2)}, u32[]{:S(2)}) collective-permute-start(bf16[64,2048]{1,0:T(8,128)(2,1)} %get-tuple-element.21), channel_id=1, source_target_pairs={{0,16},{2,18},{4,20},{6,22},{8,24},{10,26},{12,28},{14,30},{16,0},... | collective-permute-start | bytes 786440 | tf_op jit(solution)/shard_map/ppermute | solution.py:19
  322.8 51.2 %collective-permute-start.3 = (bf16[64,2048]{1,0:T(8,128)(2,1)S(1)}, bf16[64,2048]{1,0:T(8,128)(2,1)}, u32[]{:S(2)}, u32[]{:S(2)}) collective-permute-start(bf16[64,2048]{1,0:T(8,128)(2,1)S(1)} %get-tuple-element.20), channel_id=1, source_target_pairs={{0,18},{2,20},{4,22},{6,24},{8,26},{10,28},{12,30},{14,0},{16,2},{... | collective-permute-start | bytes 786440 | tf_op jit(solution)/shard_map/ppermute | solution.py:19
  358.9 17.9 %copy-start.1 = (bf16[128,2048]{1,0:T(8,128)(2,1)S(1)}, bf16[128,2048]{1,0:T(8,128)(2,1)}, u32[]{:S(2)}) copy-start(bf16[128,2048]{1,0:T(8,128)(2,1)} %param.12) | copy-start | bytes 1572868
  358.9 24.1 %copy-start.18 = (f32[128]{0:T(128)S(1)}, f32[128]{0:T(128)}, u32[]{:S(2)}) copy-start(f32[128]{0:T(128)} %get-tuple-element.32) | copy-start | bytes 1540
Sparse Core Ops, SparseCore 0:
  10.2 22.3 all-gather.5
  34.7 48.1 all-gather.9
  85.1 49.0 all-gather.7
  136.2 124.8 all-gather.11
  310.4 21.4 reduce-scatter.1
  334.1 49.6 all-gather.13

commit v2 on v1

v2 whole, which is shorter than its diff:
```python
import functools
import math

import jax
import jax.numpy as jnp
from jax import lax
from jax.experimental import pallas as pl
from jax.experimental.pallas import tpu as pltpu
from jax.sharding import PartitionSpec as P

D = 4096
HEAD = 128
GROUP = 4
TOK_DEV = 128
MAXLEN = 64
CAP = 256
TILE = 512
TILES = D // TILE
HEAD_COLS = (GROUP + 2) * HEAD
EPSILON = 1e-05
ROPE_BASE = 500000.0
BF16 = jnp.bfloat16
F32 = jnp.float32
NN = (((1,), (0,)), ((), ()))
NT = (((1,), (1,)), ((), ()))
TN = (((0,), (0,)), ((), ()))


def mm(a, b, dims=NN):
    return lax.dot_general(a, b, dims, preferred_element_type=F32)


def kernel(
    n,
    nt,
    seq_length,
    home_offset,
    dest_shard,
    dest_offset,
    hidden,
    gain,
    freq,
    cotangent,
    w_query,
    w_key,
    w_value,
    out_ref,
    gh_ref,
    gvw_ref,
    wbuf,
    hid,
    gbuf,
    nrm,
    nblk,
    ncol,
    cot_send,
    cot_recv,
    cot_home,
    acc,
    pacc,
    psend,
    precv,
    rsend,
    rrecv,
    gvbuf,
    out_send,
    out_recv,
    gvw_acc,
    load_sem,
    wsend,
    wrecv,
    ssend,
    srecv,
    gsend,
    grecv,
    gssend,
    gsrecv,
    hsend,
    hrecv,
    bsend,
    brecv,
    csend,
    crecv,
    asend,
    arecv,
    osend,
    orecv,
    psems,
    prems,
    rsems,
    rrems,
):
    me = lax.axis_index("dp")
    t = lax.axis_index("tensor")
    kh = wbuf.shape[0]
    blk = D // n
    tp = TILES // nt
    chips = n // 2
    hops = chips // 2
    zs = chips // 2
    core = lax.rem(me, 2)
    chip = lax.div(me, 2)
    z, x = lax.div(chip, 2), lax.rem(chip, 2)
    place = (1 - x) * z + x * (2 * zs - 1 - z)
    sibling = me + 1 - 2 * core
    strides = [n - 1, 1, n // 2, n // 2 + 1]

    def chip_at(position):
        position = lax.rem(position + 2 * chips, chips)
        side = lax.div(position, zs)
        return (1 - side) * (2 * position) + side * (2 * (2 * zs - 1 - position) + 1)

    sides = [chip_at(place + 1) * 2 + core, chip_at(place - 1) * 2 + core]

    barrier = pltpu.get_barrier_semaphore()

    def greet(j, carry):
        pl.semaphore_signal(
            barrier,
            inc=1,
            device_id={"dp": lax.rem(me + j, n)},
            device_id_type=pl.DeviceIdType.MESH,
        )
        return carry

    lax.fori_loop(1, n, greet, 0)
    for j in range(1, nt):
        pl.semaphore_signal(
            barrier,
            inc=1,
            device_id={"tensor": lax.rem(t + j, nt)},
            device_id_type=pl.DeviceIdType.MESH,
        )

    def remote(src, dst, ssem, rsem, where):
        return pltpu.make_async_remote_copy(
            src_ref=src,
            dst_ref=dst,
            send_sem=ssem,
            recv_sem=rsem,
            device_id=where,
            device_id_type=pl.DeviceIdType.MESH,
        )

    loads = []
    own_rows = pl.ds(pl.multiple_of(me * blk, blk), blk)
    for h in range(kh):
        for part, (src, first, width) in enumerate(
            (
                (w_query, 0, GROUP * HEAD),
                (w_key, GROUP * HEAD, HEAD),
                (w_value, (GROUP + 1) * HEAD, HEAD),
            )
        ):
            loads.append(
                pltpu.make_async_copy(
                    src.at[:, pl.ds(h * width, width)],
                    wbuf.at[h, own_rows, pl.ds(first, width)],
                    load_sem.at[h, part],
                )
            )
    for load in loads:
        load.start()

    for i in range(tp):
        hid[t * tp + i] = hidden[:, i * TILE : (i + 1) * TILE]
        gbuf[t * tp + i] = jnp.broadcast_to(gain[:, i * TILE : (i + 1) * TILE], (8, TILE))

    pl.semaphore_wait(barrier, n - 1 + nt - 1)

    own_tiles = pl.ds(t * tp, tp)
    tensor_copies = []
    for j in range(1, nt):
        peer = {"tensor": lax.rem(t + j, nt)}
        tensor_copies.append(
            remote(hid.at[own_tiles], hid.at[own_tiles], hsend.at[j, 0], hrecv.at[j, 0], peer)
        )
        tensor_copies.append(
            remote(gbuf.at[own_tiles], gbuf.at[own_tiles], hsend.at[j, 1], hrecv.at[j, 1], peer)
        )
    for copy in tensor_copies:
        copy.start()

    def w_view(h, which, q, part):
        rows = (2 * q + which) * blk
        if part is None:
            return wbuf.at[h, pl.ds(pl.multiple_of(rows, blk), blk)]
        half = blk // 2
        return wbuf.at[h, pl.ds(pl.multiple_of(rows + part * half, half), half)]

    def g_view(h, which, q, part):
        rows = (2 * q + which) * TOK_DEV
        half = TOK_DEV if part is None else TOK_DEV // 2
        rows = rows if part is None else rows + part * half
        return gvbuf.at[:, pl.ds(pl.multiple_of(rows, half), half)]

    def part_of(way, k):
        return way if k == hops else None

    def distant(way, k):
        return chip_at(place - k) if way == 0 else chip_at(place + k)

    def ring_copy(view, sems, h, way, k, q):
        block = view(h, core, q, part_of(way, k))
        return remote(
            block, block, sems[0].at[h, way, k], sems[1].at[h, way, k], {"dp": sides[way]}
        )

    def sibling_copy(view, sems, h, way, k, q, which):
        block = view(h, which, q, part_of(way, k))
        return remote(
            block, block, sems[2].at[h, way, k], sems[3].at[h, way, k], {"dp": sibling}
        )

    def ring_begin(view, sems, h):
        for way in range(2):
            ring_copy(view, sems, h, way, 1, chip).start()
        sibling_copy(view, sems, h, 0, 0, chip, core).start()

    def ring_steps(view, sems, h):
        for k in range(1, hops + 1):
            for way in range(2):
                q = distant(way, k)
                ring_copy(view, sems, h, way, k, q).wait_recv()
                if k < hops:
                    ring_copy(view, sems, h, way, k + 1, q).start()
                sibling_copy(view, sems, h, way, k, q, core).start()
        sibling_copy(view, sems, h, 0, 0, chip, 1 - core).wait_recv()
        for k in range(1, hops + 1):
            for way in range(2):
                sibling_copy(view, sems, h, way, k, distant(way, k), 1 - core).wait_recv()

    def ring_end(view, sems, h):
        sibling_copy(view, sems, h, 0, 0, chip, core).wait_send()
        for k in range(1, hops + 1):
            for way in range(2):
                q = distant(way, k)
                sibling_copy(view, sems, h, way, k, q, core).wait_send()
                ring_copy(view, sems, h, way, k, distant(way, k - 1)).wait_send()

    w_sems = (wsend, wrecv, ssend, srecv)
    g_sems = (gsend, grecv, gssend, gsrecv)
    for load in loads:
        load.wait()
    ring_begin(w_view, w_sems, 0)
    if kh > 1:
        ring_begin(w_view, w_sems, 1)

    def picked(table, row, target, slot):
        total = jnp.int32(0)
        for c in range(4):
            total = total + jnp.where(dest_shard[row, c] == target, table[row, c], 0)
        return total

    home_plan, dest_plan = [], []
    for stride in strides:
        target = lax.rem(me + stride, n)
        source = lax.rem(me - stride + n, n)
        home_plan.append(
            (picked(home_offset, me, target, 0), picked(seq_length, me, target, 0))
        )
        dest_plan.append(
            (picked(dest_offset, source, me, 0), picked(seq_length, source, me, 0))
        )

    def cut(plan, rows):
        start, length = plan
        w = lax.broadcasted_iota(jnp.int32, (MAXLEN, rows), 0)
        r = lax.broadcasted_iota(jnp.int32, (MAXLEN, rows), 1)
        return jnp.where((w < length) & (r == start + w), 1.0, 0.0).astype(BF16)

    def uncut(plan, rows):
        start, length = plan
        w = lax.broadcasted_iota(jnp.int32, (rows, MAXLEN), 1)
        r = lax.broadcasted_iota(jnp.int32, (rows, MAXLEN), 0)
        return jnp.where((w < length) & (r == start + w), 1.0, 0.0).astype(BF16)

    for e in range(4):
        cot_send[e] = mm(cut(dest_plan[e], CAP), cotangent[...]).astype(BF16)
    cot_copies = [
        remote(
            cot_send.at[e],
            cot_recv.at[e],
            csend.at[e],
            crecv.at[e],
            {"dp": lax.rem(me - strides[e] + n, n)},
        )
        for e in range(4)
    ]
    for copy in cot_copies:
        copy.start()

    for copy in tensor_copies:
        copy.wait_send()
    for j in range(1, nt):
        theirs = pl.ds(lax.rem(t - j + nt, nt) * tp, tp)
        peer = {"tensor": lax.rem(t + j, nt)}
        remote(hid.at[theirs], hid.at[theirs], hsend.at[j, 0], hrecv.at[j, 0], peer).wait_recv()
        remote(gbuf.at[theirs], gbuf.at[theirs], hsend.at[j, 1], hrecv.at[j, 1], peer).wait_recv()
    squares = jnp.zeros((TOK_DEV, 1), F32)
    for j in range(TILES):
        values = hid[j].astype(F32)
        squares = squares + jnp.sum(values * values, 1, keepdims=True)
    inverse_rms = lax.rsqrt(squares * (1.0 / D) + EPSILON)
    for j in range(TILES):
        rows = (hid[j].astype(F32) * inverse_rms * gbuf[j, 0:1, :]).astype(BF16)
        nrm[j] = rows
        for i in range(TILE // blk):
            nblk[j * (TILE // blk) + i] = rows[:, i * blk : (i + 1) * blk]
    my_tokens = pl.ds(pl.multiple_of(me * TOK_DEV, TOK_DEV), TOK_DEV)

    def norm_copy(j):
        peer = lax.rem(me + j, n)
        return remote(
            nblk.at[peer], ncol.at[my_tokens], bsend.at[j], brecv.at[j], {"dp": peer}
        )

    def norm_start(j, carry):
        norm_copy(j).start()
        return carry

    lax.fori_loop(1, n, norm_start, 0)
    ncol[my_tokens, :] = nblk[me]

    row = lax.broadcasted_iota(jnp.int32, (TOK_DEV, TOK_DEV), 0)
    col = lax.broadcasted_iota(jnp.int32, (TOK_DEV, TOK_DEV), 1)
    row_start = jnp.zeros((TOK_DEV, TOK_DEV), jnp.int32)
    col_start = jnp.zeros((TOK_DEV, TOK_DEV), jnp.int32)
    for start, length in home_plan:
        row_start = jnp.where((row >= start) & (row < start + length), start, row_start)
        col_start = jnp.where((col >= start) & (col < start + length), start, col_start)
    bias = jnp.where((row_start == col_start) & (col <= row), 0.0, -1e30).astype(F32)
    bias = jnp.concatenate([bias] * GROUP, 0)
    angles = (row - row_start).astype(F32) * freq[0:1, :]
    cosine = jnp.cos(angles)
    sine = jnp.sin(angles) * jnp.where(col < HEAD // 2, -1.0, 1.0)

    def rotate(values, sine_part):
        return values * cosine + pltpu.roll(values, HEAD // 2, 1) * sine_part

    for copy in cot_copies:
        copy.wait()
    for h in range(kh):
        total = jnp.zeros((TOK_DEV, TILE), F32)
        for e in range(4):
            total = total + mm(
                uncut(home_plan[e], TOK_DEV), cot_recv[e, :, h * TILE : (h + 1) * TILE]
            )
        cot_home[h] = total.astype(BF16)

    for j in range(TILES):
        pacc[j] = jnp.zeros((TOK_DEV, TILE), F32)

    def out_copy(h, e):
        return remote(
            out_send.at[h, e],
            out_recv.at[h, e],
            osend.at[h, e],
            orecv.at[h, e],
            {"dp": lax.rem(me + strides[e], n)},
        )

    def one_head(h, carry):
        ring_steps(w_view, w_sems, h)

        @pl.when(h + 2 < kh)
        def _():
            ring_begin(w_view, w_sems, h + 2)

        acc[...] = jnp.zeros_like(acc)

        def project(j, carry):
            rows = pl.ds(pl.multiple_of(j * TILE, TILE), TILE)
            acc[...] += mm(nrm[j], wbuf[h, rows, :])
            return carry

        lax.fori_loop(0, TILES, project, 0)
        query = jnp.concatenate(
            [rotate(acc[:, g * HEAD : (g + 1) * HEAD], sine) for g in range(GROUP)], 0
        ).astype(BF16)
        key = rotate(acc[:, GROUP * HEAD : (GROUP + 1) * HEAD], sine).astype(BF16)
        value = acc[:, (GROUP + 1) * HEAD :].astype(BF16)
        factor = HEAD**-0.5
        scores = mm(query, key, NT) * factor + bias
        exp_terms = jnp.exp(scores - jnp.max(scores, -1, keepdims=True))
        probs = exp_terms / jnp.sum(exp_terms, -1, keepdims=True)
        probs_low = probs.astype(BF16)
        mixed = mm(probs_low, value).astype(BF16)
        cot = cot_home[h]
        grad_out = jnp.concatenate(
            [cot[:, g * HEAD : (g + 1) * HEAD] for g in range(GROUP)], 0
        )
        grad_value = mm(probs_low, grad_out, TN).astype(BF16)
        grad_probs = mm(grad_out, value, NT)
        centre = jnp.sum(grad_probs * probs, -1, keepdims=True)
        grad_scores = (probs * (grad_probs - centre) * factor).astype(BF16)
        grad_query = mm(grad_scores, key)
        grad_key = rotate(mm(grad_scores, query, TN), -sine).astype(BF16)
        attn = jnp.concatenate(
            [mixed[g * TOK_DEV : (g + 1) * TOK_DEV] for g in range(GROUP)], 1
        )
        for e in range(4):
            out_send[h, e] = mm(cut(home_plan[e], TOK_DEV), attn).astype(BF16)
            out_copy(h, e).start()
        gvbuf[h, my_tokens, :] = grad_value
        grads = jnp.concatenate(
            [
                rotate(grad_query[g * TOK_DEV : (g + 1) * TOK_DEV], -sine).astype(BF16)
                for g in range(GROUP)
            ]
            + [grad_key, grad_value],
            1,
        )

        def back(j, carry):
            rows = pl.ds(pl.multiple_of(j * TILE, TILE), TILE)
            pacc[j] += mm(grads, wbuf[h, rows, :], NT)
            return carry

        lax.fori_loop(0, TILES, back, 0)
        return carry

    lax.fori_loop(0, kh, one_head, 0)

    ring_begin(g_view, g_sems, 0)
    dots = jnp.zeros((TOK_DEV, 1), F32)
    for j in range(TILES):
        low = pacc[j].astype(BF16)
        psend[j] = low
        dots = dots + jnp.sum(
            low.astype(F32) * gbuf[j, 0:1, :] * hid[j].astype(F32), 1, keepdims=True
        )
    rsend[...] = jnp.broadcast_to(dots, (TOK_DEV, HEAD))
    term_copies = []
    for j in range(1, nt):
        to = lax.rem(t + j, nt)
        peer = {"tensor": to}
        term_copies.append(
            remote(
                psend.at[pl.ds(to * tp, tp)], precv.at[j - 1], psems.at[j], prems.at[j], peer
            )
        )
        term_copies.append(remote(rsend, rrecv.at[j - 1], rsems.at[j], rrems.at[j], peer))
    for copy in term_copies:
        copy.start()
    ring_steps(g_view, g_sems, 0)
    for copy in term_copies:
        copy.wait()
    row_dot = rsend[:, 0:1]
    for j in range(1, nt):
        row_dot = row_dot + rrecv[j - 1, :, 0:1]
    for i in range(tp):
        summed = psend[t * tp + i].astype(F32)
        for j in range(1, nt):
            summed = summed + precv[j - 1, i].astype(F32)
        weighted = summed * gbuf[t * tp + i, 0:1, :]
        gh_ref[:, i * TILE : (i + 1) * TILE] = (
            inverse_rms * weighted
            - hid[t * tp + i].astype(F32) * inverse_rms**3 * row_dot * (1.0 / D)
        ).astype(BF16)

    for h in range(kh):
        for e in range(4):
            out_copy(h, e).wait()
        total = jnp.zeros((CAP, TILE), F32)
        for e in range(4):
            total = total + mm(uncut(dest_plan[e], CAP), out_recv[h, e])
        out_ref[:, h * TILE : (h + 1) * TILE] = total.astype(BF16)

    def norm_wait(j, carry):
        peer = lax.rem(me - j + n, n)
        theirs = pl.ds(pl.multiple_of(peer * TOK_DEV, TOK_DEV), TOK_DEV)
        remote(
            nblk.at[peer], ncol.at[theirs], bsend.at[j], brecv.at[j], {"dp": peer}
        ).wait_recv()
        norm_copy(j).wait_send()
        return carry

    lax.fori_loop(1, n, norm_wait, 0)
    gvw_acc[...] = jnp.zeros_like(gvw_acc)

    def weigh(c, carry):
        rows = pl.ds(pl.multiple_of(c * TILE, TILE), TILE)
        for h in range(kh):
            gvw_acc[:, h * HEAD : (h + 1) * HEAD] += mm(ncol[rows, :], gvbuf[h, rows, :], TN)
        return carry

    lax.fori_loop(0, n * TOK_DEV // TILE, weigh, 0)
    gvw_ref[...] = gvw_acc[...]

    def finish(h, carry):
        ring_end(w_view, w_sems, h)
        return carry

    lax.fori_loop(0, kh, finish, 0)
    ring_end(g_view, g_sems, 0)


def on_device(
    hidden,
    gain,
    w_query,
    w_key,
    w_value,
    cotangent,
    seq_length,
    home_offset,
    dest_shard,
    dest_offset,
):
    n = lax.axis_size("dp")
    nt = lax.axis_size("tensor")
    kh = w_key.shape[1] // HEAD
    width = hidden.shape[1]
    blk = D // n
    tp = TILES // nt
    hops = n // 4
    half = HEAD // 2
    exponent = jnp.arange(half, dtype=F32) * (2.0 / HEAD)
    inverse = jnp.power(jnp.float32(ROPE_BASE), -exponent)
    freq = jnp.broadcast_to(jnp.concatenate([inverse, inverse])[None, :], (8, HEAD))
    dma = pltpu.SemaphoreType.DMA
    vmem = pl.BlockSpec(memory_space=pltpu.VMEM)
    smem = pl.BlockSpec(memory_space=pltpu.SMEM)
    anywhere = pl.BlockSpec(memory_space=pl.ANY)
    return pl.pallas_call(
        functools.partial(kernel, n, nt),
        out_shape=(
            jax.ShapeDtypeStruct((CAP, width), BF16),
            jax.ShapeDtypeStruct((TOK_DEV, width), BF16),
            jax.ShapeDtypeStruct((blk, kh * HEAD), F32),
        ),
        in_specs=[smem] * 4 + [vmem] * 4 + [anywhere] * 3,
        out_specs=(vmem, vmem, vmem),
        scratch_shapes=[
            pltpu.VMEM((kh, D, HEAD_COLS), BF16),
            pltpu.VMEM((TILES, TOK_DEV, TILE), BF16),
            pltpu.VMEM((TILES, 8, TILE), F32),
            pltpu.VMEM((TILES, TOK_DEV, TILE), BF16),
            pltpu.VMEM((n, TOK_DEV, blk), BF16),
            pltpu.VMEM((n * TOK_DEV, blk), BF16),
            pltpu.VMEM((4, MAXLEN, width), BF16),
            pltpu.VMEM((4, MAXLEN, width), BF16),
            pltpu.VMEM((kh, TOK_DEV, TILE), BF16),
            pltpu.VMEM((TOK_DEV, HEAD_COLS), F32),
            pltpu.VMEM((TILES, TOK_DEV, TILE), F32),
            pltpu.VMEM((TILES, TOK_DEV, TILE), BF16),
            pltpu.VMEM((nt - 1, tp, TOK_DEV, TILE), BF16),
            pltpu.VMEM((TOK_DEV, HEAD), F32),
            pltpu.VMEM((nt - 1, TOK_DEV, HEAD), F32),
            pltpu.VMEM((kh, n * TOK_DEV, HEAD), BF16),
            pltpu.VMEM((kh, 4, MAXLEN, TILE), BF16),
            pltpu.VMEM((kh, 4, MAXLEN, TILE), BF16),
            pltpu.VMEM((blk, kh * HEAD), F32),
            dma((kh, 3)),
            dma((kh, 2, hops + 1)),
            dma((kh, 2, hops + 1)),
            dma((kh, 2, hops + 1)),
            dma((kh, 2, hops + 1)),
            dma((1, 2, hops + 1)),
            dma((1, 2, hops + 1)),
            dma((1, 2, hops + 1)),
            dma((1, 2, hops + 1)),
            dma((nt, 2)),
            dma((nt, 2)),
            dma((n,)),
            dma((n,)),
            dma((4,)),
            dma((4,)),
            dma((4,)),
            dma((4,)),
            dma((kh, 4)),
            dma((kh, 4)),
            dma((nt,)),
            dma((nt,)),
            dma((nt,)),
            dma((nt,)),
        ],
        compiler_params=pltpu.CompilerParams(
            collective_id=0, has_side_effects=True, vmem_limit_bytes=56 * 1024 * 1024
        ),
        cost_estimate=pl.CostEstimate(
            flops=8 * 10**9, bytes_accessed=8 * 10**6, transcendentals=10**6
        ),
    )(
        seq_length,
        home_offset,
        dest_shard,
        dest_offset,
        hidden,
        gain.astype(F32)[None, :],
        freq,
        cotangent,
        w_query,
        w_key,
        w_value,
    )


def solution(mesh):
    return jax.shard_map(
        on_device,
        mesh=mesh,
        in_specs=(
            P("dp", "tensor"),
            P("tensor"),
            P("dp", "tensor"),
            P("dp", "tensor"),
            P("dp", "tensor"),
            P("dp", "tensor"),
            P(),
            P(),
            P(),
            P(),
        ),
        out_specs=(P("dp", "tensor"), P("dp", "tensor"), P("dp", "tensor")),
        check_vma=False,
    )
```

time: 401 us -> 260 us (0.65)
  the two profiles are of different devices: /device:TPU:26 before, /device:TPU:1 now
where the time goes in v2:
time: 260 us; the launch traced here: 259 us
  Pallas kernels  250 us (96%)
  local copies, waits for them, and re-layouts  7.81 us (3%)
    pallas_call x1, Pallas kernels, on_device(): pl.pallas_call(functools.partial(kernel, n, nt), out_shape=(jax.ShapeDtyp...  250 us
    unnamed x21, local copies, waits for them, and re-layouts  7.2 us

profile of v2, /device:TPU:1, one launch (start us, length us, event | category | flops | bytes accessed | tf_op | source)
XLA Modules:
  0.0 259.3 jit_solution(15609733166833126298)
XLA Ops:
  0.6 0.0 copy-start.2
  0.7 0.1 pad_maximum_fusion
  0.7 0.6 broadcast_in_dim.13.freq
  1.3 0.0 copy-done.2
  1.3 0.0 copy-start.3
  1.3 0.6 broadcast_in_dim.14
  1.9 0.1 copy-done.3
  2.0 0.0 copy-start.4
  2.0 0.7 copy.13.seq_length
  2.7 0.0 copy-done.4
  2.7 0.0 copy-start.5
  2.7 0.7 copy.14.home_offset
  3.4 0.0 copy-done.5
  3.4 0.0 copy-start.6
  3.4 0.7 copy.15.dest_shard
  4.1 0.0 copy-done.6
  4.1 0.7 copy.16.dest_offset
  4.8 250.1 %shard_map.121 = (bf16[256,2048]{1,0:T(8,128)(2,1)}, bf16[128,2048]{1,0:T(8,128)(2,1)}, f32[256,512]{1,0:T(8,128)}) custom-call(s32[16,4]{1,0:T(8,128)} %copy.13.seq_length, s32[16,4]{1,0:T(8,128)} %copy.14.home_offset, s32[16,4]{1,0:T(8,128)} %copy.15.dest_shard, s32[16,4]{1,0:T(8,128)} %copy.16.dest_offset, bf16[128,2048]{1,0:T(8,128)(2,1)} %hidden.1, ...), custom_call_target="tpu_custom_call" | custom-call | flops 8000000000 | bytes 8000000 | tf_op jit(solution)/shard_map/pallas_call | solution.py:526
  254.9 0.0 copy-start.1
  254.9 2.4 copy.20
  257.3 0.0 copy-done.1
  257.3 0.0 copy-start
  257.3 0.8 copy.21
  258.1 0.4 copy-done
  258.5 0.8 copy.22
  (1 shorter events, 0.0 us)
Async XLA Ops:
  0.6 0.7 copy-start.2
  1.3 0.7 copy-start.3
  2.0 0.7 copy-start.4
  2.7 0.7 copy-start.5
  3.4 0.7 copy-start.6
  254.9 2.4 copy-start.1
  257.3 1.2 copy-start

commit v3 on v2

--- a/solution.py
+++ b/solution.py
@@ -67,14 +67,20 @@
     out_recv,
     gvw_acc,
     load_sem,
-    wsend,
-    wrecv,
-    ssend,
-    srecv,
-    gsend,
-    grecv,
-    gssend,
-    gsrecv,
+    wzs,
+    wzr,
+    wxs,
+    wxr,
+    wss,
+    wsr,
+    gzs,
+    gzr,
+    gxs,
+    gxr,
+    gss,
+    gsr,
+    ysend,
+    yrecv,
     hsend,
     hrecv,
     bsend,
@@ -95,22 +101,12 @@
     kh = wbuf.shape[0]
     blk = D // n
     tp = TILES // nt
-    chips = n // 2
-    hops = chips // 2
-    zs = chips // 2
+    zs = n // 4
     core = lax.rem(me, 2)
     chip = lax.div(me, 2)
     z, x = lax.div(chip, 2), lax.rem(chip, 2)
-    place = (1 - x) * z + x * (2 * zs - 1 - z)
     sibling = me + 1 - 2 * core
     strides = [n - 1, 1, n // 2, n // 2 + 1]
-
-    def chip_at(position):
-        position = lax.rem(position + 2 * chips, chips)
-        side = lax.div(position, zs)
-        return (1 - side) * (2 * position) + side * (2 * (2 * zs - 1 - position) + 1)
-
-    sides = [chip_at(place + 1) * 2 + core, chip_at(place - 1) * 2 + core]
 
     barrier = pltpu.get_barrier_semaphore()
 
@@ -181,70 +177,126 @@
     for copy in tensor_copies:
         copy.start()
 
-    def w_view(h, which, q, part):
-        rows = (2 * q + which) * blk
-        if part is None:
-            return wbuf.at[h, pl.ds(pl.multiple_of(rows, blk), blk)]
-        half = blk // 2
-        return wbuf.at[h, pl.ds(pl.multiple_of(rows + part * half, half), half)]
-
-    def g_view(h, which, q, part):
-        rows = (2 * q + which) * TOK_DEV
-        half = TOK_DEV if part is None else TOK_DEV // 2
-        rows = rows if part is None else rows + part * half
-        return gvbuf.at[:, pl.ds(pl.multiple_of(rows, half), half)]
-
-    def part_of(way, k):
-        return way if k == hops else None
-
-    def distant(way, k):
-        return chip_at(place - k) if way == 0 else chip_at(place + k)
-
-    def ring_copy(view, sems, h, way, k, q):
-        block = view(h, core, q, part_of(way, k))
+    def w_view(h, zz, xx, which):
+        rows = pl.multiple_of((4 * zz + 2 * xx + which) * blk, blk)
+        return wbuf.at[h, pl.ds(rows, blk)]
+
+    def g_view(h, zz, xx, which):
+        rows = pl.multiple_of((4 * zz + 2 * xx + which) * TOK_DEV, TOK_DEV)
+        return gvbuf.at[h, pl.ds(rows, TOK_DEV)]
+
+    up, down = lax.rem(me + 4, n), lax.rem(me - 4 + n, n)
+    across = me + 2 - 4 * x
+
+    def z_copy(view, sems, h, way, zz):
+        block = view(h, zz, x, core)
         return remote(
-            block, block, sems[0].at[h, way, k], sems[1].at[h, way, k], {"dp": sides[way]}
-        )
-
-    def sibling_copy(view, sems, h, way, k, q, which):
-        block = view(h, which, q, part_of(way, k))
+            block,
+            block,
+            sems[0].at[h, way, zz],
+            sems[1].at[h, zz],
+            {"dp": up if way == 0 else down},
+        )
+
+    def x_copy(view, sems, h, zz, xx):
+        block = view(h, zz, xx, core)
+        return remote(block, block, sems[2].at[h, zz], sems[3].at[h, zz], {"dp": across})
+
+    def s_copy(view, sems, h, zz, xx, which):
+        block = view(h, zz, xx, which)
         return remote(
-            block, block, sems[2].at[h, way, k], sems[3].at[h, way, k], {"dp": sibling}
-        )
-
-    def ring_begin(view, sems, h):
-        for way in range(2):
-            ring_copy(view, sems, h, way, 1, chip).start()
-        sibling_copy(view, sems, h, 0, 0, chip, core).start()
-
-    def ring_steps(view, sems, h):
-        for k in range(1, hops + 1):
-            for way in range(2):
-                q = distant(way, k)
-                ring_copy(view, sems, h, way, k, q).wait_recv()
-                if k < hops:
-                    ring_copy(view, sems, h, way, k + 1, q).start()
-                sibling_copy(view, sems, h, way, k, q, core).start()
-        sibling_copy(view, sems, h, 0, 0, chip, 1 - core).wait_recv()
-        for k in range(1, hops + 1):
-            for way in range(2):
-                sibling_copy(view, sems, h, way, k, distant(way, k), 1 - core).wait_recv()
-
-    def ring_end(view, sems, h):
-        sibling_copy(view, sems, h, 0, 0, chip, core).wait_send()
-        for k in range(1, hops + 1):
-            for way in range(2):
-                q = distant(way, k)
-                sibling_copy(view, sems, h, way, k, q, core).wait_send()
-                ring_copy(view, sems, h, way, k, distant(way, k - 1)).wait_send()
-
-    w_sems = (wsend, wrecv, ssend, srecv)
-    g_sems = (gsend, grecv, gssend, gsrecv)
+            block, block, sems[4].at[h, xx, zz], sems[5].at[h, xx, zz], {"dp": sibling}
+        )
+
+    def begin(view, sems, h):
+        @pl.when(z < zs - 1)
+        def _():
+            z_copy(view, sems, h, 0, z).start()
+
+        @pl.when(z > 0)
+        def _():
+            z_copy(view, sems, h, 1, z).start()
+
+        x_copy(view, sems, h, z, x).start()
+        s_copy(view, sems, h, z, x, core).start()
+
+    def step(view, sems, h, k):
+        if k < zs:
+
+            @pl.when(z >= k)
+            def _():
+                zz = z - k
+                z_copy(view, sems, h, 0, zz).wait_recv()
+
+                @pl.when(z < zs - 1)
+                def _():
+                    z_copy(view, sems, h, 0, zz).start()
+
+                x_copy(view, sems, h, zz, x).start()
+                s_copy(view, sems, h, zz, x, core).start()
+
+            @pl.when(z + k < zs)
+            def _():
+                zz = z + k
+                z_copy(view, sems, h, 1, zz).wait_recv()
+
+                @pl.when(z > 0)
+                def _():
+                    z_copy(view, sems, h, 1, zz).start()
+
+                x_copy(view, sems, h, zz, x).start()
+                s_copy(view, sems, h, zz, x, core).start()
+
+        def from_across(zz):
+            x_copy(view, sems, h, zz, 1 - x).wait_recv()
+            s_copy(view, sems, h, zz, 1 - x, core).start()
+
+        if k == 1:
+            from_across(z)
+        else:
+
+            @pl.when(z >= k - 1)
+            def _():
+                from_across(z - k + 1)
+
+            @pl.when(z + k - 1 < zs)
+            def _():
+                from_across(z + k - 1)
+
+    def gathered(view, sems, h):
+        def one(zz, carry):
+            s_copy(view, sems, h, zz, x, 1 - core).wait_recv()
+            s_copy(view, sems, h, zz, 1 - x, 1 - core).wait_recv()
+            return carry
+
+        lax.fori_loop(0, zs, one, 0)
+
+    def drained(view, sems, h):
+        def one(zz, carry):
+            s_copy(view, sems, h, zz, x, core).wait_send()
+            s_copy(view, sems, h, zz, 1 - x, core).wait_send()
+            x_copy(view, sems, h, zz, x).wait_send()
+
+            @pl.when((zz <= z) & (z < zs - 1))
+            def _():
+                z_copy(view, sems, h, 0, zz).wait_send()
+
+            @pl.when((zz >= z) & (z > 0))
+            def _():
+                z_copy(view, sems, h, 1, zz).wait_send()
+
+            return carry
+
+        lax.fori_loop(0, zs, one, 0)
+
+    w_sems = (wzs, wzr, wxs, wxr, wss, wsr)
+    g_sems = (gzs, gzr, gxs, gxr, gss, gsr)
+    early = zs // 2
     for load in loads:
         load.wait()
-    ring_begin(w_view, w_sems, 0)
+    begin(w_view, w_sems, 0)
     if kh > 1:
-        ring_begin(w_view, w_sems, 1)
+        begin(w_view, w_sems, 1)
 
     def picked(table, row, target, slot):
         total = jnp.int32(0)
@@ -289,6 +341,8 @@
     ]
     for copy in cot_copies:
         copy.start()
+    for k in range(1, early):
+        step(w_view, w_sems, 0, k)
 
     for copy in tensor_copies:
         copy.wait_send()
@@ -308,19 +362,43 @@
         for i in range(TILE // blk):
             nblk[j * (TILE // blk) + i] = rows[:, i * blk : (i + 1) * blk]
     my_tokens = pl.ds(pl.multiple_of(me * TOK_DEV, TOK_DEV), TOK_DEV)
-
-    def norm_copy(j):
-        peer = lax.rem(me + j, n)
+    share = TOK_DEV // nt
+    my_share = pl.ds(pl.multiple_of(t * share, share), share)
+
+    def norm_copy(j, src, dst):
         return remote(
-            nblk.at[peer], ncol.at[my_tokens], bsend.at[j], brecv.at[j], {"dp": peer}
+            nblk.at[src, my_share],
+            ncol.at[dst, my_share],
+            bsend.at[j],
+            brecv.at[j],
+            {"dp": lax.rem(me + j, n)},
         )
 
     def norm_start(j, carry):
-        norm_copy(j).start()
+        norm_copy(j, lax.rem(me + j, n), me).start()
         return carry
 
     lax.fori_loop(1, n, norm_start, 0)
-    ncol[my_tokens, :] = nblk[me]
+    ncol[me, my_share, :] = nblk[me, my_share, :]
+
+    def share_copy(j, shard):
+        rows = pl.ds(pl.multiple_of(shard * share, share), share)
+        block = ncol.at[:, rows]
+        return remote(
+            block, block, ysend.at[j], yrecv.at[j], {"tensor": lax.rem(t + j, nt)}
+        )
+
+    def share_rows():
+        def norm_wait(j, carry):
+            norm_copy(j, lax.rem(me + j, n), lax.rem(me - j + n, n)).wait_recv()
+            norm_copy(j, lax.rem(me + j, n), me).wait_send()
+            return carry
+
+        lax.fori_loop(1, n, norm_wait, 0)
+        for j in range(1, nt):
+            share_copy(j, t).start()
+
+    step(w_view, w_sems, 0, early)
 
     row = lax.broadcasted_iota(jnp.int32, (TOK_DEV, TOK_DEV), 0)
     col = lax.broadcasted_iota(jnp.int32, (TOK_DEV, TOK_DEV), 1)
@@ -360,13 +438,8 @@
             {"dp": lax.rem(me + strides[e], n)},
         )
 
-    def one_head(h, carry):
-        ring_steps(w_view, w_sems, h)
-
-        @pl.when(h + 2 < kh)
-        def _():
-            ring_begin(w_view, w_sems, h + 2)
-
+    def project_head(h):
+        gathered(w_view, w_sems, h)
         acc[...] = jnp.zeros_like(acc)
 
         def project(j, carry):
@@ -375,6 +448,7 @@
             return carry
 
         lax.fori_loop(0, TILES, project, 0)
+    def attend_head(h):
         query = jnp.concatenate(
             [rotate(acc[:, g * HEAD : (g + 1) * HEAD], sine) for g in range(GROUP)], 0
         ).astype(BF16)
@@ -418,11 +492,47 @@
             return carry
 
         lax.fori_loop(0, TILES, back, 0)
+        begin(g_view, g_sems, h)
+
+    def round_of(h, carry):
+        for k in range(1, early + 1):
+
+            @pl.when(h < kh)
+            def _():
+                step(w_view, w_sems, h, early + k)
+
+            @pl.when(h + 1 < kh)
+            def _():
+                step(w_view, w_sems, h + 1, k)
+
+            @pl.when((h >= 2) & (h < kh))
+            def _():
+                step(g_view, g_sems, h - 2, 2 * k - 1)
+                step(g_view, g_sems, h - 2, 2 * k)
+
+            if k == 1:
+
+                @pl.when(h + 2 < kh)
+                def _():
+                    begin(w_view, w_sems, h + 2)
+
+                @pl.when(h >= 1)
+                def _():
+                    project_head(h - 1)
+
+        @pl.when(h >= 1)
+        def _():
+            attend_head(h - 1)
+
+        @pl.when(h == 1)
+        def _():
+            share_rows()
+
         return carry
 
-    lax.fori_loop(0, kh, one_head, 0)
-
-    ring_begin(g_view, g_sems, 0)
+    lax.fori_loop(0, kh + 1, round_of, 0)
+
+    last = range(max(kh - 2, 0), kh)
     dots = jnp.zeros((TOK_DEV, 1), F32)
     for j in range(TILES):
         low = pacc[j].astype(BF16)
@@ -443,7 +553,19 @@
         term_copies.append(remote(rsend, rrecv.at[j - 1], rsems.at[j], rrems.at[j], peer))
     for copy in term_copies:
         copy.start()
-    ring_steps(g_view, g_sems, 0)
+    def place_out(h):
+        for e in range(4):
+            out_copy(h, e).wait()
+        total = jnp.zeros((CAP, TILE), F32)
+        for e in range(4):
+            total = total + mm(uncut(dest_plan[e], CAP), out_recv[h, e])
+        out_ref[:, h * TILE : (h + 1) * TILE] = total.astype(BF16)
+
+    for k in range(1, zs + 1):
+        for h in last:
+            step(g_view, g_sems, h, k)
+        if k <= kh:
+            place_out(k - 1)
     for copy in term_copies:
         copy.wait()
     row_dot = rsend[:, 0:1]
@@ -459,41 +581,30 @@
             - hid[t * tp + i].astype(F32) * inverse_rms**3 * row_dot * (1.0 / D)
         ).astype(BF16)
 
+    for j in range(1, nt):
+        share_copy(j, t).wait_send()
+        share_copy(j, lax.rem(t - j + nt, nt)).wait_recv()
     for h in range(kh):
-        for e in range(4):
-            out_copy(h, e).wait()
-        total = jnp.zeros((CAP, TILE), F32)
-        for e in range(4):
-            total = total + mm(uncut(dest_plan[e], CAP), out_recv[h, e])
-        out_ref[:, h * TILE : (h + 1) * TILE] = total.astype(BF16)
-
-    def norm_wait(j, carry):
-        peer = lax.rem(me - j + n, n)
-        theirs = pl.ds(pl.multiple_of(peer * TOK_DEV, TOK_DEV), TOK_DEV)
-        remote(
-            nblk.at[peer], ncol.at[theirs], bsend.at[j], brecv.at[j], {"dp": peer}
-        ).wait_recv()
-        norm_copy(j).wait_send()
-        return carry
-
-    lax.fori_loop(1, n, norm_wait, 0)
+        gathered(g_view, g_sems, h)
     gvw_acc[...] = jnp.zeros_like(gvw_acc)
 
     def weigh(c, carry):
         rows = pl.ds(pl.multiple_of(c * TILE, TILE), TILE)
-        for h in range(kh):
-            gvw_acc[:, h * HEAD : (h + 1) * HEAD] += mm(ncol[rows, :], gvbuf[h, rows, :], TN)
+        owners = pl.ds(c * (TILE // TOK_DEV), TILE // TOK_DEV)
+        columns = ncol[owners].reshape(TILE, blk)
+        values = jnp.concatenate([gvbuf[h, rows, :] for h in range(kh)], 1)
+        gvw_acc[...] += mm(columns, values, TN)
         return carry
 
     lax.fori_loop(0, n * TOK_DEV // TILE, weigh, 0)
     gvw_ref[...] = gvw_acc[...]
 
     def finish(h, carry):
-        ring_end(w_view, w_sems, h)
+        drained(w_view, w_sems, h)
+        drained(g_view, g_sems, h)
         return carry
 
     lax.fori_loop(0, kh, finish, 0)
-    ring_end(g_view, g_sems, 0)
 
 
 def on_device(
@@ -514,7 +625,7 @@
     width = hidden.shape[1]
     blk = D // n
     tp = TILES // nt
-    hops = n // 4
+    zs = n // 4
     half = HEAD // 2
     exponent = jnp.arange(half, dtype=F32) * (2.0 / HEAD)
     inverse = jnp.power(jnp.float32(ROPE_BASE), -exponent)
@@ -538,7 +649,7 @@
             pltpu.VMEM((TILES, 8, TILE), F32),
             pltpu.VMEM((TILES, TOK_DEV, TILE), BF16),
             pltpu.VMEM((n, TOK_DEV, blk), BF16),
-            pltpu.VMEM((n * TOK_DEV, blk), BF16),
+            pltpu.VMEM((n, TOK_DEV, blk), BF16),
             pltpu.VMEM((4, MAXLEN, width), BF16),
             pltpu.VMEM((4, MAXLEN, width), BF16),
             pltpu.VMEM((kh, TOK_DEV, TILE), BF16),
@@ -553,14 +664,20 @@
             pltpu.VMEM((kh, 4, MAXLEN, TILE), BF16),
             pltpu.VMEM((blk, kh * HEAD), F32),
             dma((kh, 3)),
-            dma((kh, 2, hops + 1)),
-            dma((kh, 2, hops + 1)),
-            dma((kh, 2, hops + 1)),
-            dma((kh, 2, hops + 1)),
-            dma((1, 2, hops + 1)),
-            dma((1, 2, hops + 1)),
-            dma((1, 2, hops + 1)),
-            dma((1, 2, hops + 1)),
+            dma((kh, 2, zs)),
+            dma((kh, zs)),
+            dma((kh, zs)),
+            dma((kh, zs)),
+            dma((kh, 2, zs)),
+            dma((kh, 2, zs)),
+            dma((kh, 2, zs)),
+            dma((kh, zs)),
+            dma((kh, zs)),
+            dma((kh, zs)),
+            dma((kh, 2, zs)),
+            dma((kh, 2, zs)),
+            dma((nt,)),
+            dma((nt,)),
             dma((nt, 2)),
             dma((nt, 2)),
             dma((n,)),

time: 260 us -> 241 us (0.927)
  the two profiles are of different devices: /device:TPU:1 before, /device:TPU:26 now
where the time goes in v3:
time: 241 us; the launch traced here: 238 us
  Pallas kernels  229 us (95%)
  local copies, waits for them, and re-layouts  7.81 us (3%)
    pallas_call x1, Pallas kernels, on_device(): pl.pallas_call(functools.partial(kernel, n, nt), out_shape=(jax.ShapeDtyp...  229 us
    unnamed x21, local copies, waits for them, and re-layouts  7.2 us

profile of v3, /device:TPU:26, one launch (start us, length us, event | category | flops | bytes accessed | tf_op | source)
XLA Modules:
  0.0 237.7 jit_solution(12767144624944263671)
XLA Ops:
  0.6 0.0 copy-start.2
  0.7 0.1 pad_maximum_fusion
  0.7 0.6 broadcast_in_dim.13.freq
  1.3 0.0 copy-done.2
  1.3 0.0 copy-start.3
  1.3 0.6 broadcast_in_dim.14
  1.9 0.1 copy-done.3
  2.0 0.0 copy-start.4
  2.0 0.7 copy.13.seq_length
  2.7 0.0 copy-done.4
  2.7 0.0 copy-start.5
  2.7 0.7 copy.14.home_offset
  3.4 0.0 copy-done.5
  3.4 0.0 copy-start.6
  3.4 0.7 copy.15.dest_shard
  4.1 0.0 copy-done.6
  4.1 0.7 copy.16.dest_offset
  4.8 228.6 %shard_map.121 = (bf16[256,2048]{1,0:T(8,128)(2,1)}, bf16[128,2048]{1,0:T(8,128)(2,1)}, f32[256,512]{1,0:T(8,128)}) custom-call(s32[16,4]{1,0:T(8,128)} %copy.13.seq_length, s32[16,4]{1,0:T(8,128)} %copy.14.home_offset, s32[16,4]{1,0:T(8,128)} %copy.15.dest_shard, s32[16,4]{1,0:T(8,128)} %copy.16.dest_offset, bf16[128,2048]{1,0:T(8,128)(2,1)} %hidden.1, ...), custom_call_target="tpu_custom_call" | custom-call | flops 8000000000 | bytes 8000000 | tf_op jit(solution)/shard_map/pallas_call | solution.py:637
  233.3 0.0 copy-start.1
  233.3 2.4 copy.20
  235.7 0.0 copy-done.1
  235.7 0.0 copy-start
  235.7 0.8 copy.21
  236.5 0.4 copy-done
  236.9 0.8 copy.22
  (1 shorter events, 0.0 us)
Async XLA Ops:
  0.6 0.7 copy-start.2
  1.3 0.7 copy-start.3
  2.0 0.7 copy-start.4
  2.7 0.7 copy-start.5
  3.4 0.7 copy-start.6
  233.3 2.4 copy-start.1
  235.7 1.2 copy-start

commit v4 on v3

--- a/solution.py
+++ b/solution.py
@@ -57,6 +57,7 @@
     cot_recv,
     cot_home,
     acc,
+    grads_t,
     pacc,
     psend,
     precv,
@@ -294,9 +295,8 @@
     early = zs // 2
     for load in loads:
         load.wait()
-    begin(w_view, w_sems, 0)
-    if kh > 1:
-        begin(w_view, w_sems, 1)
+    for h in range(kh):
+        begin(w_view, w_sems, h)
 
     def picked(table, row, target, slot):
         total = jnp.int32(0)
@@ -316,19 +316,31 @@
         )
 
     def cut(plan, rows):
-        start, length = plan
         w = lax.broadcasted_iota(jnp.int32, (MAXLEN, rows), 0)
         r = lax.broadcasted_iota(jnp.int32, (MAXLEN, rows), 1)
-        return jnp.where((w < length) & (r == start + w), 1.0, 0.0).astype(BF16)
+        return jnp.concatenate(
+            [
+                jnp.where((w < length) & (r == start + w), 1.0, 0.0)
+                for start, length in plan
+            ],
+            0,
+        ).astype(BF16)
 
     def uncut(plan, rows):
-        start, length = plan
-        w = lax.broadcasted_iota(jnp.int32, (rows, MAXLEN), 1)
-        r = lax.broadcasted_iota(jnp.int32, (rows, MAXLEN), 0)
-        return jnp.where((w < length) & (r == start + w), 1.0, 0.0).astype(BF16)
-
-    for e in range(4):
-        cot_send[e] = mm(cut(dest_plan[e], CAP), cotangent[...]).astype(BF16)
+        place = lax.broadcasted_iota(jnp.int32, (rows, 4 * MAXLEN), 1)
+        r = lax.broadcasted_iota(jnp.int32, (rows, 4 * MAXLEN), 0)
+        total = jnp.zeros((rows, 4 * MAXLEN), F32)
+        for e, (start, length) in enumerate(plan):
+            w = place - e * MAXLEN
+            total = jnp.where((w >= 0) & (w < length) & (r == start + w), 1.0, total)
+        return total.astype(BF16)
+
+    picks = cut(dest_plan, CAP)
+    for i in range(tp):
+        columns = slice(i * TILE, (i + 1) * TILE)
+        cot_send[:, :, columns] = (
+            mm(picks, cotangent[:, columns]).astype(BF16).reshape(4, MAXLEN, TILE)
+        )
     cot_copies = [
         remote(
             cot_send.at[e],
@@ -418,16 +430,13 @@
 
     for copy in cot_copies:
         copy.wait()
+    picks = uncut(home_plan, TOK_DEV)
     for h in range(kh):
-        total = jnp.zeros((TOK_DEV, TILE), F32)
-        for e in range(4):
-            total = total + mm(
-                uncut(home_plan[e], TOK_DEV), cot_recv[e, :, h * TILE : (h + 1) * TILE]
-            )
-        cot_home[h] = total.astype(BF16)
+        arrived = cot_recv[:, :, h * TILE : (h + 1) * TILE].reshape(4 * MAXLEN, TILE)
+        cot_home[h] = mm(picks, arrived).astype(BF16)
 
     for j in range(TILES):
-        pacc[j] = jnp.zeros((TOK_DEV, TILE), F32)
+        pacc[j] = jnp.zeros((TILE, TOK_DEV), F32)
 
     def out_copy(h, e):
         return remote(
@@ -438,16 +447,14 @@
             {"dp": lax.rem(me + strides[e], n)},
         )
 
-    def project_head(h):
-        gathered(w_view, w_sems, h)
-        acc[...] = jnp.zeros_like(acc)
-
+    def project_head(h, first, last):
         def project(j, carry):
             rows = pl.ds(pl.multiple_of(j * TILE, TILE), TILE)
             acc[...] += mm(nrm[j], wbuf[h, rows, :])
             return carry
 
-        lax.fori_loop(0, TILES, project, 0)
+        lax.fori_loop(first, last, project, 0)
+
     def attend_head(h):
         query = jnp.concatenate(
             [rotate(acc[:, g * HEAD : (g + 1) * HEAD], sine) for g in range(GROUP)], 0
@@ -464,35 +471,39 @@
         grad_out = jnp.concatenate(
             [cot[:, g * HEAD : (g + 1) * HEAD] for g in range(GROUP)], 0
         )
-        grad_value = mm(probs_low, grad_out, TN).astype(BF16)
+        grad_value = mm(probs_low, grad_out, TN)
         grad_probs = mm(grad_out, value, NT)
         centre = jnp.sum(grad_probs * probs, -1, keepdims=True)
         grad_scores = (probs * (grad_probs - centre) * factor).astype(BF16)
         grad_query = mm(grad_scores, key)
-        grad_key = rotate(mm(grad_scores, query, TN), -sine).astype(BF16)
+        grad_key = rotate(mm(grad_scores, query, TN), -sine)
         attn = jnp.concatenate(
             [mixed[g * TOK_DEV : (g + 1) * TOK_DEV] for g in range(GROUP)], 1
         )
+        out_send[h] = (
+            mm(cut(home_plan, TOK_DEV), attn).astype(BF16).reshape(4, MAXLEN, TILE)
+        )
         for e in range(4):
-            out_send[h, e] = mm(cut(home_plan[e], TOK_DEV), attn).astype(BF16)
             out_copy(h, e).start()
-        gvbuf[h, my_tokens, :] = grad_value
+        gvbuf[h, my_tokens, :] = grad_value.astype(BF16)
         grads = jnp.concatenate(
             [
-                rotate(grad_query[g * TOK_DEV : (g + 1) * TOK_DEV], -sine).astype(BF16)
+                rotate(grad_query[g * TOK_DEV : (g + 1) * TOK_DEV], -sine).T
                 for g in range(GROUP)
             ]
-            + [grad_key, grad_value],
-            1,
-        )
-
+            + [grad_key.T, grad_value.T],
+            0,
+        )
+        grads_t[...] = grads.astype(BF16)
+        begin(g_view, g_sems, h)
+
+    def back_head(h):
         def back(j, carry):
             rows = pl.ds(pl.multiple_of(j * TILE, TILE), TILE)
-            pacc[j] += mm(grads, wbuf[h, rows, :], NT)
+            pacc[j] += mm(wbuf[h, rows, :], grads_t[...])
             return carry
 
         lax.fori_loop(0, TILES, back, 0)
-        begin(g_view, g_sems, h)
 
     def round_of(h, carry):
         for k in range(1, early + 1):
@@ -501,10 +512,6 @@
             def _():
                 step(w_view, w_sems, h, early + k)
 
-            @pl.when(h + 1 < kh)
-            def _():
-                step(w_view, w_sems, h + 1, k)
-
             @pl.when((h >= 2) & (h < kh))
             def _():
                 step(g_view, g_sems, h - 2, 2 * k - 1)
@@ -512,17 +519,33 @@
 
             if k == 1:
 
-                @pl.when(h + 2 < kh)
-                def _():
-                    begin(w_view, w_sems, h + 2)
-
                 @pl.when(h >= 1)
                 def _():
-                    project_head(h - 1)
-
-        @pl.when(h >= 1)
-        def _():
-            attend_head(h - 1)
+                    gathered(w_view, w_sems, h - 1)
+                    acc[...] = jnp.zeros_like(acc)
+                    project_head(h - 1, 0, TILES // 2)
+
+            if k == 2:
+
+                @pl.when(h >= 1)
+                def _():
+                    attend_head(h - 1)
+
+            @pl.when(h + 1 < kh)
+            def _():
+                step(w_view, w_sems, h + 1, k)
+
+            if k == 1:
+
+                @pl.when(h >= 1)
+                def _():
+                    project_head(h - 1, TILES // 2, TILES)
+
+            if k == 2:
+
+                @pl.when(h >= 1)
+                def _():
+                    back_head(h - 1)
 
         @pl.when(h == 1)
         def _():
@@ -535,7 +558,7 @@
     last = range(max(kh - 2, 0), kh)
     dots = jnp.zeros((TOK_DEV, 1), F32)
     for j in range(TILES):
-        low = pacc[j].astype(BF16)
+        low = pacc[j].T.astype(BF16)
         psend[j] = low
         dots = dots + jnp.sum(
             low.astype(F32) * gbuf[j, 0:1, :] * hid[j].astype(F32), 1, keepdims=True
@@ -556,10 +579,8 @@
     def place_out(h):
         for e in range(4):
             out_copy(h, e).wait()
-        total = jnp.zeros((CAP, TILE), F32)
-        for e in range(4):
-            total = total + mm(uncut(dest_plan[e], CAP), out_recv[h, e])
-        out_ref[:, h * TILE : (h + 1) * TILE] = total.astype(BF16)
+        arrived = out_recv[h].reshape(4 * MAXLEN, TILE)
+        out_ref[:, h * TILE : (h + 1) * TILE] = mm(uncut(dest_plan, CAP), arrived).astype(BF16)
 
     for k in range(1, zs + 1):
         for h in last:
@@ -654,7 +675,8 @@
             pltpu.VMEM((4, MAXLEN, width), BF16),
             pltpu.VMEM((kh, TOK_DEV, TILE), BF16),
             pltpu.VMEM((TOK_DEV, HEAD_COLS), F32),
-            pltpu.VMEM((TILES, TOK_DEV, TILE), F32),
+            pltpu.VMEM((HEAD_COLS, TOK_DEV), BF16),
+            pltpu.VMEM((TILES, TILE, TOK_DEV), F32),
             pltpu.VMEM((TILES, TOK_DEV, TILE), BF16),
             pltpu.VMEM((nt - 1, tp, TOK_DEV, TILE), BF16),
             pltpu.VMEM((TOK_DEV, HEAD), F32),

time: 241 us -> 239 us (level)
  Pallas kernels: 229 us -> 226 us
    pallas_call x1, Pallas kernels: 229 us -> 226 us  [on_device(): pl.pallas_call(functools.partial(kernel, n, nt), out_shape=(jax.ShapeDtyp...]
where the time goes in v4:
time: 239 us; the launch traced here: 235 us
  Pallas kernels  226 us (95%)
  local copies, waits for them, and re-layouts  7.81 us (3%)
    pallas_call x1, Pallas kernels, on_device(): pl.pallas_call(functools.partial(kernel, n, nt), out_shape=(jax.ShapeDtyp...  226 us
    unnamed x21, local copies, waits for them, and re-layouts  7.2 us

profile of v4, /device:TPU:26, one launch (start us, length us, event | category | flops | bytes accessed | tf_op | source)
XLA Modules:
  0.0 234.9 jit_solution(12450619935228972621)
XLA Ops:
  0.6 0.0 copy-start.2
  0.7 0.1 pad_maximum_fusion
  0.7 0.6 broadcast_in_dim.13.freq
  1.3 0.0 copy-done.2
  1.3 0.0 copy-start.3
  1.3 0.6 broadcast_in_dim.14
  1.9 0.1 copy-done.3
  2.0 0.0 copy-start.4
  2.0 0.7 copy.13.seq_length
  2.7 0.0 copy-done.4
  2.7 0.0 copy-start.5
  2.7 0.7 copy.14.home_offset
  3.4 0.0 copy-done.5
  3.4 0.0 copy-start.6
  3.4 0.7 copy.15.dest_shard
  4.1 0.0 copy-done.6
  4.1 0.7 copy.16.dest_offset
  4.8 225.8 %shard_map.121 = (bf16[256,2048]{1,0:T(8,128)(2,1)}, bf16[128,2048]{1,0:T(8,128)(2,1)}, f32[256,512]{1,0:T(8,128)}) custom-call(s32[16,4]{1,0:T(8,128)} %copy.13.seq_length, s32[16,4]{1,0:T(8,128)} %copy.14.home_offset, s32[16,4]{1,0:T(8,128)} %copy.15.dest_shard, s32[16,4]{1,0:T(8,128)} %copy.16.dest_offset, bf16[128,2048]{1,0:T(8,128)(2,1)} %hidden.1, ...), custom_call_target="tpu_custom_call" | custom-call | flops 8000000000 | bytes 8000000 | tf_op jit(solution)/shard_map/pallas_call | solution.py:658
  230.5 0.0 copy-start.1
  230.6 2.4 %copy.20 = bf16[256,2048]{1,0:T(8,128)(2,1)} copy(bf16[256,2048]{1,0:T(8,128)(2,1)} %get-tuple-element.6) | data formatting | bytes 2097152
  232.9 0.0 copy-done.1
  232.9 0.0 copy-start
  232.9 0.8 copy.21
  233.7 0.4 copy-done
  234.2 0.8 copy.22
  (1 shorter events, 0.0 us)
Async XLA Ops:
  0.6 0.7 copy-start.2
  1.3 0.7 copy-start.3
  2.0 0.7 copy-start.4
  2.7 0.7 copy-start.5
  3.4 0.7 copy-start.6
  230.5 2.4 %copy-start.1 = (bf16[128,2048]{1,0:T(8,128)(2,1)S(1)}, bf16[128,2048]{1,0:T(8,128)(2,1)}, u32[]{:S(2)}) copy-start(bf16[128,2048]{1,0:T(8,128)(2,1)} %get-tuple-element.7) | copy-start | bytes 1572868
  232.9 1.2 copy-start

commit v5 on v4

--- a/solution.py
+++ b/solution.py
@@ -626,6 +626,726 @@
         return carry
 
     lax.fori_loop(0, kh, finish, 0)
+
+
+def split_kernel(
+    n,
+    nt,
+    seq_length,
+    home_offset,
+    dest_shard,
+    dest_offset,
+    hidden,
+    gain,
+    freq,
+    cotangent,
+    w_query,
+    w_key,
+    w_value,
+    out_ref,
+    gh_ref,
+    gvw_ref,
+    wbuf,
+    hid,
+    gbuf,
+    cosines,
+    sines,
+    biases,
+    cot_across,
+    attn_out,
+    attn_in,
+    pxs,
+    pxr,
+    nblk,
+    ncol,
+    cot_send,
+    cot_recv,
+    cot_home,
+    acc,
+    grads_t,
+    pacc,
+    psend,
+    precv,
+    rsend,
+    rrecv,
+    gvbuf,
+    out_send,
+    out_recv,
+    gvw_acc,
+    load_sem,
+    wzs,
+    wzr,
+    wxs,
+    wxr,
+    wss,
+    wsr,
+    gzs,
+    gzr,
+    gxs,
+    gxr,
+    gss,
+    gsr,
+    ysend,
+    yrecv,
+    ysends,
+    yrecvs,
+    qsend,
+    qrecv,
+    hsend,
+    hrecv,
+    bsend,
+    brecv,
+    csend,
+    crecv,
+    asend,
+    arecv,
+    osend,
+    orecv,
+    psems,
+    prems,
+    rsems,
+    rrems,
+):
+    me = lax.axis_index("dp")
+    t = lax.axis_index("tensor")
+    kh = gvbuf.shape[0]
+    hh = kh // 2
+    blk = D // n
+    tp = TILES // nt
+    zs = n // 4
+    core = lax.rem(me, 2)
+    chip = lax.div(me, 2)
+    z, x = lax.div(chip, 2), lax.rem(chip, 2)
+    sibling = me + 1 - 2 * core
+    across = me + 2 - 4 * x
+    spot = 4 * z + 2 * core + x
+    other_spot = spot + 1 - 2 * x
+    strides = [n - 1, 1, n // 2, n // 2 + 1]
+
+    barrier = pltpu.get_barrier_semaphore()
+
+    def greet(j, carry):
+        pl.semaphore_signal(
+            barrier,
+            inc=1,
+            device_id={"dp": lax.rem(me + j, n)},
+            device_id_type=pl.DeviceIdType.MESH,
+        )
+        return carry
+
+    lax.fori_loop(1, n, greet, 0)
+    for j in range(1, nt):
+        pl.semaphore_signal(
+            barrier,
+            inc=1,
+            device_id={"tensor": lax.rem(t + j, nt)},
+            device_id_type=pl.DeviceIdType.MESH,
+        )
+
+    def remote(src, dst, ssem, rsem, where):
+        return pltpu.make_async_remote_copy(
+            src_ref=src,
+            dst_ref=dst,
+            send_sem=ssem,
+            recv_sem=rsem,
+            device_id=where,
+            device_id_type=pl.DeviceIdType.MESH,
+        )
+
+    def shard_parts(h, which):
+        head = which * hh + h
+        for part, (src, first, width) in enumerate(
+            (
+                (w_query, 0, GROUP * HEAD),
+                (w_key, GROUP * HEAD, HEAD),
+                (w_value, (GROUP + 1) * HEAD, HEAD),
+            )
+        ):
+            yield part, src.at[:, pl.ds(pl.multiple_of(head * width, width), width)], pl.ds(
+                first, width
+            )
+
+    def rows_at(where):
+        return pl.ds(pl.multiple_of(where * blk, blk), blk)
+
+    def loads_of(h):
+        return [
+            pltpu.make_async_copy(src, wbuf.at[h, rows_at(spot), cols], load_sem.at[h, part])
+            for part, src, cols in shard_parts(h, x)
+        ]
+
+    def swaps_of(h, where):
+        return [
+            remote(
+                src,
+                wbuf.at[h, rows_at(where), cols],
+                wxs.at[h, part],
+                wxr.at[h, part],
+                {"dp": across},
+            )
+            for part, src, cols in shard_parts(h, 1 - x)
+        ]
+
+    for h in range(hh):
+        for load in loads_of(h):
+            load.start()
+
+    for i in range(tp):
+        hid[t * tp + i] = hidden[:, i * TILE : (i + 1) * TILE]
+        gbuf[t * tp + i] = jnp.broadcast_to(gain[:, i * TILE : (i + 1) * TILE], (8, TILE))
+
+    pl.semaphore_wait(barrier, n - 1 + nt - 1)
+
+    for h in range(hh):
+        for swap in swaps_of(h, spot):
+            swap.start()
+
+    own_tiles = pl.ds(t * tp, tp)
+    tensor_copies = []
+    for j in range(1, nt):
+        peer = {"tensor": lax.rem(t + j, nt)}
+        tensor_copies.append(
+            remote(hid.at[own_tiles], hid.at[own_tiles], hsend.at[j, 0], hrecv.at[j, 0], peer)
+        )
+        tensor_copies.append(
+            remote(gbuf.at[own_tiles], gbuf.at[own_tiles], hsend.at[j, 1], hrecv.at[j, 1], peer)
+        )
+    for copy in tensor_copies:
+        copy.start()
+
+    def w_view(h, zz, xx, which):
+        rows = pl.multiple_of((4 * zz + 2 * which) * blk, 2 * blk)
+        return wbuf.at[h, pl.ds(rows, 2 * blk)]
+
+    def g_view(h, zz, xx, which):
+        rows = pl.multiple_of((4 * zz + 2 * which) * TOK_DEV, 2 * TOK_DEV)
+        return gvbuf.at[xx * hh + h, pl.ds(rows, 2 * TOK_DEV)]
+
+    up, down = lax.rem(me + 4, n), lax.rem(me - 4 + n, n)
+
+    def z_copy(view, sems, h, way, zz):
+        block = view(h, zz, x, core)
+        return remote(
+            block,
+            block,
+            sems[0].at[h, way, zz],
+            sems[1].at[h, zz],
+            {"dp": up if way == 0 else down},
+        )
+
+    def x_copy(view, sems, h, zz, xx):
+        block = view(h, zz, xx, core)
+        return remote(block, block, sems[2].at[h, zz], sems[3].at[h, zz], {"dp": across})
+
+    def s_copy(view, sems, h, zz, xx, which):
+        block = view(h, zz, xx, which)
+        return remote(
+            block, block, sems[4].at[h, xx, zz], sems[5].at[h, xx, zz], {"dp": sibling}
+        )
+
+    def begin(view, sems, h):
+        @pl.when(z < zs - 1)
+        def _():
+            z_copy(view, sems, h, 0, z).start()
+
+        @pl.when(z > 0)
+        def _():
+            z_copy(view, sems, h, 1, z).start()
+
+        if sems is g_sems:
+            x_copy(view, sems, h, z, x).start()
+        s_copy(view, sems, h, z, x, core).start()
+
+    def step(view, sems, h, k):
+        if k < zs:
+
+            @pl.when(z >= k)
+            def _():
+                zz = z - k
+                z_copy(view, sems, h, 0, zz).wait_recv()
+
+                @pl.when(z < zs - 1)
+                def _():
+                    z_copy(view, sems, h, 0, zz).start()
+
+                if sems is g_sems:
+                    x_copy(view, sems, h, zz, x).start()
+                s_copy(view, sems, h, zz, x, core).start()
+
+            @pl.when(z + k < zs)
+            def _():
+                zz = z + k
+                z_copy(view, sems, h, 1, zz).wait_recv()
+
+                @pl.when(z > 0)
+                def _():
+                    z_copy(view, sems, h, 1, zz).start()
+
+                if sems is g_sems:
+                    x_copy(view, sems, h, zz, x).start()
+                s_copy(view, sems, h, zz, x, core).start()
+
+        if sems is w_sems:
+            return
+
+        def from_across(zz):
+            x_copy(view, sems, h, zz, 1 - x).wait_recv()
+            s_copy(view, sems, h, zz, 1 - x, core).start()
+
+        if k == 1:
+            from_across(z)
+        else:
+
+            @pl.when(z >= k - 1)
+            def _():
+                from_across(z - k + 1)
+
+            @pl.when(z + k - 1 < zs)
+            def _():
+                from_across(z + k - 1)
+
+    def gathered(view, sems, h):
+        def one(zz, carry):
+            s_copy(view, sems, h, zz, x, 1 - core).wait_recv()
+            if sems is g_sems:
+                s_copy(view, sems, h, zz, 1 - x, 1 - core).wait_recv()
+            return carry
+
+        lax.fori_loop(0, zs, one, 0)
+
+    def drained(view, sems, h):
+        def one(zz, carry):
+            s_copy(view, sems, h, zz, x, core).wait_send()
+            if sems is g_sems:
+                s_copy(view, sems, h, zz, 1 - x, core).wait_send()
+                x_copy(view, sems, h, zz, x).wait_send()
+
+            @pl.when((zz <= z) & (z < zs - 1))
+            def _():
+                z_copy(view, sems, h, 0, zz).wait_send()
+
+            @pl.when((zz >= z) & (z > 0))
+            def _():
+                z_copy(view, sems, h, 1, zz).wait_send()
+
+            return carry
+
+        lax.fori_loop(0, zs, one, 0)
+
+    w_sems = (wzs, wzr, None, None, wss, wsr)
+    g_sems = (gzs, gzr, gxs, gxr, gss, gsr)
+    early = zs // 2
+    def begin_weights(h):
+        for load in loads_of(h):
+            load.wait()
+        for swap in swaps_of(h, other_spot):
+            swap.wait_recv()
+        begin(w_view, w_sems, h)
+
+    begin_weights(0)
+
+    def picked(table, row, target, slot):
+        total = jnp.int32(0)
+        for c in range(4):
+            total = total + jnp.where(dest_shard[row, c] == target, table[row, c], 0)
+        return total
+
+    home_plan, dest_plan, across_plan = [], [], []
+    for stride in strides:
+        target = lax.rem(across + stride, n)
+        across_plan.append(
+            (
+                picked(home_offset, across, target, 0),
+                picked(seq_length, across, target, 0),
+            )
+        )
+        target = lax.rem(me + stride, n)
+        source = lax.rem(me - stride + n, n)
+        home_plan.append(
+            (picked(home_offset, me, target, 0), picked(seq_length, me, target, 0))
+        )
+        dest_plan.append(
+            (picked(dest_offset, source, me, 0), picked(seq_length, source, me, 0))
+        )
+
+    def cut(plan, rows):
+        w = lax.broadcasted_iota(jnp.int32, (MAXLEN, rows), 0)
+        r = lax.broadcasted_iota(jnp.int32, (MAXLEN, rows), 1)
+        return jnp.concatenate(
+            [
+                jnp.where((w < length) & (r == start + w), 1.0, 0.0)
+                for start, length in plan
+            ],
+            0,
+        ).astype(BF16)
+
+    def uncut(plan, rows):
+        place = lax.broadcasted_iota(jnp.int32, (rows, 4 * MAXLEN), 1)
+        r = lax.broadcasted_iota(jnp.int32, (rows, 4 * MAXLEN), 0)
+        total = jnp.zeros((rows, 4 * MAXLEN), F32)
+        for e, (start, length) in enumerate(plan):
+            w = place - e * MAXLEN
+            total = jnp.where((w >= 0) & (w < length) & (r == start + w), 1.0, total)
+        return total.astype(BF16)
+
+    picks = cut(dest_plan, CAP)
+    for i in range(tp):
+        columns = slice(i * TILE, (i + 1) * TILE)
+        cot_send[:, :, columns] = (
+            mm(picks, cotangent[:, columns]).astype(BF16).reshape(4, MAXLEN, TILE)
+        )
+    cot_copies = [
+        remote(
+            cot_send.at[e],
+            cot_recv.at[e],
+            csend.at[e],
+            crecv.at[e],
+            {"dp": lax.rem(me - strides[e] + n, n)},
+        )
+        for e in range(4)
+    ]
+    for copy in cot_copies:
+        copy.start()
+    for h in range(1, hh):
+        begin_weights(h)
+    for k in range(1, early):
+        step(w_view, w_sems, 0, k)
+
+    for copy in tensor_copies:
+        copy.wait_send()
+    for j in range(1, nt):
+        theirs = pl.ds(lax.rem(t - j + nt, nt) * tp, tp)
+        peer = {"tensor": lax.rem(t + j, nt)}
+        remote(hid.at[theirs], hid.at[theirs], hsend.at[j, 0], hrecv.at[j, 0], peer).wait_recv()
+        remote(gbuf.at[theirs], gbuf.at[theirs], hsend.at[j, 1], hrecv.at[j, 1], peer).wait_recv()
+    squares = jnp.zeros((TOK_DEV, 1), F32)
+    for j in range(TILES):
+        values = hid[j].astype(F32)
+        squares = squares + jnp.sum(values * values, 1, keepdims=True)
+    inverse_rms = lax.rsqrt(squares * (1.0 / D) + EPSILON)
+    for j in range(TILES):
+        rows = (hid[j].astype(F32) * inverse_rms * gbuf[j, 0:1, :]).astype(BF16)
+        for i in range(TILE // blk):
+            nblk[x, j * (TILE // blk) + i] = rows[:, i * blk : (i + 1) * blk]
+    row_swap = remote(nblk.at[x], nblk.at[x], qsend.at[0], qrecv.at[0], {"dp": across})
+    row_swap.start()
+    share = TOK_DEV // nt
+    my_share = pl.ds(pl.multiple_of(t * share, share), share)
+
+    def norm_copy(j, src, dst):
+        return remote(
+            nblk.at[x, src, my_share],
+            ncol.at[dst, my_share],
+            bsend.at[j],
+            brecv.at[j],
+            {"dp": lax.rem(me + j, n)},
+        )
+
+    def norm_start(j, carry):
+        norm_copy(j, lax.rem(me + j, n), spot).start()
+        return carry
+
+    lax.fori_loop(1, n, norm_start, 0)
+    ncol[spot, my_share, :] = nblk[x, me, my_share, :]
+
+    def share_copy(j, shard):
+        rows = pl.ds(pl.multiple_of(shard * share, share), share)
+        block = ncol.at[:, rows]
+        return remote(
+            block, block, ysend.at[j], yrecv.at[j], {"tensor": lax.rem(t + j, nt)}
+        )
+
+    def share_rows():
+        def norm_wait(j, carry):
+            sender = lax.rem(me - j + n, n)
+            side = lax.rem(sender, 4)
+            where = sender - side + 2 * lax.rem(side, 2) + lax.div(side, 2)
+            norm_copy(j, lax.rem(me + j, n), where).wait_recv()
+            norm_copy(j, lax.rem(me + j, n), spot).wait_send()
+            return carry
+
+        lax.fori_loop(1, n, norm_wait, 0)
+        for j in range(1, nt):
+            share_copy(j, t).start()
+
+    step(w_view, w_sems, 0, early)
+
+    row = lax.broadcasted_iota(jnp.int32, (TOK_DEV, TOK_DEV), 0)
+    col = lax.broadcasted_iota(jnp.int32, (TOK_DEV, TOK_DEV), 1)
+
+    def tables(plan):
+        row_start = jnp.zeros((TOK_DEV, TOK_DEV), jnp.int32)
+        col_start = jnp.zeros((TOK_DEV, TOK_DEV), jnp.int32)
+        for start, length in plan:
+            row_start = jnp.where((row >= start) & (row < start + length), start, row_start)
+            col_start = jnp.where((col >= start) & (col < start + length), start, col_start)
+        bias = jnp.where((row_start == col_start) & (col <= row), 0.0, -1e30).astype(F32)
+        angles = (row - row_start).astype(F32) * freq[0:1, :]
+        sine = jnp.sin(angles) * jnp.where(col < HEAD // 2, -1.0, 1.0)
+        return jnp.cos(angles), sine, jnp.concatenate([bias] * GROUP, 0)
+
+    for side, plan in enumerate((home_plan, across_plan)):
+        cosines[side], sines[side], biases[side] = tables(plan)
+
+    def rotate(values, cosine, sine_part):
+        return values * cosine + pltpu.roll(values, HEAD // 2, 1) * sine_part
+
+    for copy in cot_copies:
+        copy.wait()
+    picks = uncut(home_plan, TOK_DEV)
+    for h in range(kh):
+        arrived = cot_recv[:, :, h * TILE : (h + 1) * TILE].reshape(4 * MAXLEN, TILE)
+        cot_home[h] = mm(picks, arrived).astype(BF16)
+
+    cot_swap = remote(
+        cot_home.at[pl.ds((1 - x) * hh, hh)], cot_across, qsend.at[1], qrecv.at[1], {"dp": across}
+    )
+    cot_swap.start()
+
+    for j in range(n):
+        pacc[j] = jnp.zeros((blk, 2 * TOK_DEV), F32)
+    cot_swap.wait()
+    row_swap.wait()
+
+    def out_copy(h, e):
+        return remote(
+            out_send.at[h, e],
+            out_recv.at[h, e],
+            osend.at[h, e],
+            orecv.at[h, e],
+            {"dp": lax.rem(me + strides[e], n)},
+        )
+
+    def project_head(h, first, last):
+        def project(j, carry):
+            side = lax.rem(j, 4)
+            shard = j - side + 2 * lax.rem(side, 2) + lax.div(side, 2)
+            rows = pl.ds(pl.multiple_of(j * blk, blk), blk)
+            both = jnp.concatenate([nblk[x, shard], nblk[1 - x, shard]], 0)
+            acc[...] += mm(both, wbuf[h, rows, :])
+            return carry
+
+        lax.fori_loop(first, last, project, 0)
+
+    def attn_copy(h):
+        return remote(
+            attn_out.at[h], attn_in.at[h], ysends.at[h], yrecvs.at[h], {"dp": across}
+        )
+
+    def send_out(head, attn):
+        out_send[head] = (
+            mm(cut(home_plan, TOK_DEV), attn).astype(BF16).reshape(4, MAXLEN, TILE)
+        )
+        for e in range(4):
+            out_copy(head, e).start()
+
+    def attend_side(h, side, where):
+        first = side * TOK_DEV
+        rows = slice(first, first + TOK_DEV)
+        cosine, sine = cosines[side], sines[side]
+        query = jnp.concatenate(
+            [
+                rotate(acc[rows, g * HEAD : (g + 1) * HEAD], cosine, sine)
+                for g in range(GROUP)
+            ],
+            0,
+        ).astype(BF16)
+        key = rotate(acc[rows, GROUP * HEAD : (GROUP + 1) * HEAD], cosine, sine).astype(BF16)
+        value = acc[rows, (GROUP + 1) * HEAD :].astype(BF16)
+        factor = HEAD**-0.5
+        scores = mm(query, key, NT) * factor + biases[side]
+        exp_terms = jnp.exp(scores - jnp.max(scores, -1, keepdims=True))
+        probs = exp_terms / jnp.sum(exp_terms, -1, keepdims=True)
+        probs_low = probs.astype(BF16)
+        mixed = mm(probs_low, value).astype(BF16)
+        cot = cot_home[x * hh + h] if side == 0 else cot_across[h]
+        grad_out = jnp.concatenate(
+            [cot[:, g * HEAD : (g + 1) * HEAD] for g in range(GROUP)], 0
+        )
+        grad_value = mm(probs_low, grad_out, TN)
+        grad_probs = mm(grad_out, value, NT)
+        centre = jnp.sum(grad_probs * probs, -1, keepdims=True)
+        grad_scores = (probs * (grad_probs - centre) * factor).astype(BF16)
+        grad_query = mm(grad_scores, key)
+        grad_key = rotate(mm(grad_scores, query, TN), cosine, -sine)
+        attn = jnp.concatenate(
+            [mixed[g * TOK_DEV : (g + 1) * TOK_DEV] for g in range(GROUP)], 1
+        )
+        if side == 0:
+            send_out(x * hh + h, attn)
+        else:
+            attn_out[h] = attn
+            attn_copy(h).start()
+        tokens = pl.ds(pl.multiple_of(where * TOK_DEV, TOK_DEV), TOK_DEV)
+        gvbuf[x * hh + h, tokens, :] = grad_value.astype(BF16)
+        grads = jnp.concatenate(
+            [
+                rotate(grad_query[g * TOK_DEV : (g + 1) * TOK_DEV], cosine, -sine).T
+                for g in range(GROUP)
+            ]
+            + [grad_key.T, grad_value.T],
+            0,
+        )
+        grads_t[:, rows] = grads.astype(BF16)
+
+    def attend_head(h):
+        attend_side(h, 1, other_spot)
+        attend_side(h, 0, spot)
+        begin(g_view, g_sems, h)
+
+    def from_other(h):
+        attn_copy(h).wait()
+        send_out((1 - x) * hh + h, attn_in[h])
+
+    def back_head(h):
+        def back(j, carry):
+            rows = pl.ds(pl.multiple_of(j * blk, blk), blk)
+            pacc[j] += mm(wbuf[h, rows, :], grads_t[...])
+            return carry
+
+        lax.fori_loop(0, n, back, 0)
+
+    def round_of(h, carry):
+        for k in range(1, early + 1):
+
+            @pl.when(h < hh)
+            def _():
+                step(w_view, w_sems, h, early + k)
+
+            @pl.when((h >= 2) & (h < hh))
+            def _():
+                step(g_view, g_sems, h - 2, 2 * k - 1)
+                step(g_view, g_sems, h - 2, 2 * k)
+
+            if k == 1:
+
+                @pl.when(h >= 1)
+                def _():
+                    gathered(w_view, w_sems, h - 1)
+                    acc[...] = jnp.zeros_like(acc)
+                    project_head(h - 1, 0, n // 2)
+
+            if k == 2:
+
+                @pl.when(h >= 1)
+                def _():
+                    attend_head(h - 1)
+
+            @pl.when(h + 1 < hh)
+            def _():
+                step(w_view, w_sems, h + 1, k)
+
+            if k == 1:
+
+                @pl.when(h >= 1)
+                def _():
+                    project_head(h - 1, n // 2, n)
+
+            if k == 2:
+
+                @pl.when(h >= 1)
+                def _():
+                    back_head(h - 1)
+
+        @pl.when(h >= 2)
+        def _():
+            from_other(h - 2)
+
+        @pl.when(h == 1)
+        def _():
+            share_rows()
+
+        return carry
+
+    lax.fori_loop(0, hh + 1, round_of, 0)
+
+    last = range(max(hh - 2, 0), hh)
+    for j in range(n):
+        pxs[j] = pacc[j, :, TOK_DEV:].astype(BF16)
+    half_swap = remote(pxs, pxr, qsend.at[2], qrecv.at[2], {"dp": across})
+    half_swap.start()
+    from_other(hh - 1)
+    for h in last:
+        step(g_view, g_sems, h, 1)
+    half_swap.wait()
+    for j in range(n):
+        total = pacc[j, :, :TOK_DEV] + pxr[j].astype(F32)
+        shard = j - j % 4 + 2 * (j % 2) + (j % 4) // 2
+        first = shard * blk % TILE
+        psend[shard * blk // TILE, :, first : first + blk] = total.T.astype(BF16)
+    dots = jnp.zeros((TOK_DEV, 1), F32)
+    for j in range(TILES):
+        low = psend[j]
+        dots = dots + jnp.sum(
+            low.astype(F32) * gbuf[j, 0:1, :] * hid[j].astype(F32), 1, keepdims=True
+        )
+    rsend[...] = jnp.broadcast_to(dots, (TOK_DEV, HEAD))
+    term_copies = []
+    for j in range(1, nt):
+        to = lax.rem(t + j, nt)
+        peer = {"tensor": to}
+        term_copies.append(
+            remote(
+                psend.at[pl.ds(to * tp, tp)], precv.at[j - 1], psems.at[j], prems.at[j], peer
+            )
+        )
+        term_copies.append(remote(rsend, rrecv.at[j - 1], rsems.at[j], rrems.at[j], peer))
+    for copy in term_copies:
+        copy.start()
+    def place_out(h):
+        for e in range(4):
+            out_copy(h, e).wait()
+        arrived = out_recv[h].reshape(4 * MAXLEN, TILE)
+        out_ref[:, h * TILE : (h + 1) * TILE] = mm(uncut(dest_plan, CAP), arrived).astype(BF16)
+
+    for k in range(1, zs + 1):
+        for h in last:
+            if k > 1:
+                step(g_view, g_sems, h, k)
+        if k <= kh:
+            place_out(k - 1)
+    for copy in term_copies:
+        copy.wait()
+    row_dot = rsend[:, 0:1]
+    for j in range(1, nt):
+        row_dot = row_dot + rrecv[j - 1, :, 0:1]
+    for i in range(tp):
+        summed = psend[t * tp + i].astype(F32)
+        for j in range(1, nt):
+            summed = summed + precv[j - 1, i].astype(F32)
+        weighted = summed * gbuf[t * tp + i, 0:1, :]
+        gh_ref[:, i * TILE : (i + 1) * TILE] = (
+            inverse_rms * weighted
+            - hid[t * tp + i].astype(F32) * inverse_rms**3 * row_dot * (1.0 / D)
+        ).astype(BF16)
+
+    for j in range(1, nt):
+        share_copy(j, t).wait_send()
+        share_copy(j, lax.rem(t - j + nt, nt)).wait_recv()
+    for h in range(hh):
+        gathered(g_view, g_sems, h)
+    gvw_acc[...] = jnp.zeros_like(gvw_acc)
+
+    def weigh(c, carry):
+        rows = pl.ds(pl.multiple_of(c * TILE, TILE), TILE)
+        owners = pl.ds(c * (TILE // TOK_DEV), TILE // TOK_DEV)
+        columns = ncol[owners].reshape(TILE, blk)
+        values = jnp.concatenate([gvbuf[h, rows, :] for h in range(kh)], 1)
+        gvw_acc[...] += mm(columns, values, TN)
+        return carry
+
+    lax.fori_loop(0, n * TOK_DEV // TILE, weigh, 0)
+    gvw_ref[...] = gvw_acc[...]
+
+    def finish(h, carry):
+        drained(w_view, w_sems, h)
+        drained(g_view, g_sems, h)
+        return carry
+
+    lax.fori_loop(0, hh, finish, 0)
+    for h in range(hh):
+        for swap in swaps_of(h, spot):
+            swap.wait_send()
 
 
 def on_device(
@@ -736,9 +1456,133 @@
     )
 
 
+def on_split_device(
+    hidden,
+    gain,
+    w_query,
+    w_key,
+    w_value,
+    cotangent,
+    seq_length,
+    home_offset,
+    dest_shard,
+    dest_offset,
+):
+    n = lax.axis_size("dp")
+    nt = lax.axis_size("tensor")
+    kh = w_key.shape[1] // HEAD
+    hh = kh // 2
+    width = hidden.shape[1]
+    blk = D // n
+    tp = TILES // nt
+    zs = n // 4
+    half = HEAD // 2
+    exponent = jnp.arange(half, dtype=F32) * (2.0 / HEAD)
+    inverse = jnp.power(jnp.float32(ROPE_BASE), -exponent)
+    freq = jnp.broadcast_to(jnp.concatenate([inverse, inverse])[None, :], (8, HEAD))
+    dma = pltpu.SemaphoreType.DMA
+    vmem = pl.BlockSpec(memory_space=pltpu.VMEM)
+    smem = pl.BlockSpec(memory_space=pltpu.SMEM)
+    anywhere = pl.BlockSpec(memory_space=pl.ANY)
+    return pl.pallas_call(
+        functools.partial(split_kernel, n, nt),
+        out_shape=(
+            jax.ShapeDtypeStruct((CAP, width), BF16),
+            jax.ShapeDtypeStruct((TOK_DEV, width), BF16),
+            jax.ShapeDtypeStruct((blk, kh * HEAD), F32),
+        ),
+        in_specs=[smem] * 4 + [vmem] * 4 + [anywhere] * 3,
+        out_specs=(vmem, vmem, vmem),
+        scratch_shapes=[
+            pltpu.VMEM((hh, D, HEAD_COLS), BF16),
+            pltpu.VMEM((TILES, TOK_DEV, TILE), BF16),
+            pltpu.VMEM((TILES, 8, TILE), F32),
+            pltpu.VMEM((2, TOK_DEV, HEAD), F32),
+            pltpu.VMEM((2, TOK_DEV, HEAD), F32),
+            pltpu.VMEM((2, GROUP * TOK_DEV, TOK_DEV), F32),
+            pltpu.VMEM((hh, TOK_DEV, TILE), BF16),
+            pltpu.VMEM((hh, TOK_DEV, TILE), BF16),
+            pltpu.VMEM((hh, TOK_DEV, TILE), BF16),
+            pltpu.VMEM((n, blk, TOK_DEV), BF16),
+            pltpu.VMEM((n, blk, TOK_DEV), BF16),
+            pltpu.VMEM((2, n, TOK_DEV, blk), BF16),
+            pltpu.VMEM((n, TOK_DEV, blk), BF16),
+            pltpu.VMEM((4, MAXLEN, width), BF16),
+            pltpu.VMEM((4, MAXLEN, width), BF16),
+            pltpu.VMEM((kh, TOK_DEV, TILE), BF16),
+            pltpu.VMEM((2 * TOK_DEV, HEAD_COLS), F32),
+            pltpu.VMEM((HEAD_COLS, 2 * TOK_DEV), BF16),
+            pltpu.VMEM((n, blk, 2 * TOK_DEV), F32),
+            pltpu.VMEM((TILES, TOK_DEV, TILE), BF16),
+            pltpu.VMEM((nt - 1, tp, TOK_DEV, TILE), BF16),
+            pltpu.VMEM((TOK_DEV, HEAD), F32),
+            pltpu.VMEM((nt - 1, TOK_DEV, HEAD), F32),
+            pltpu.VMEM((kh, n * TOK_DEV, HEAD), BF16),
+            pltpu.VMEM((kh, 4, MAXLEN, TILE), BF16),
+            pltpu.VMEM((kh, 4, MAXLEN, TILE), BF16),
+            pltpu.VMEM((blk, kh * HEAD), F32),
+            dma((kh, 3)),
+            dma((kh, 2, zs)),
+            dma((kh, zs)),
+            dma((kh, max(zs, 3))),
+            dma((kh, max(zs, 3))),
+            dma((kh, 2, zs)),
+            dma((kh, 2, zs)),
+            dma((kh, 2, zs)),
+            dma((kh, zs)),
+            dma((kh, zs)),
+            dma((kh, zs)),
+            dma((kh, 2, zs)),
+            dma((kh, 2, zs)),
+            dma((nt,)),
+            dma((nt,)),
+            dma((hh,)),
+            dma((hh,)),
+            dma((3,)),
+            dma((3,)),
+            dma((nt, 2)),
+            dma((nt, 2)),
+            dma((n,)),
+            dma((n,)),
+            dma((4,)),
+            dma((4,)),
+            dma((4,)),
+            dma((4,)),
+            dma((kh, 4)),
+            dma((kh, 4)),
+            dma((nt,)),
+            dma((nt,)),
+            dma((nt,)),
+            dma((nt,)),
+        ],
+        compiler_params=pltpu.CompilerParams(
+            collective_id=1, has_side_effects=True, vmem_limit_bytes=56 * 1024 * 1024
+        ),
+        cost_estimate=pl.CostEstimate(
+            flops=8 * 10**9, bytes_accessed=8 * 10**6, transcendentals=10**6
+        ),
+    )(
+        seq_length,
+        home_offset,
+        dest_shard,
+        dest_offset,
+        hidden,
+        gain.astype(F32)[None, :],
+        freq,
+        cotangent,
+        w_query,
+        w_key,
+        w_value,
+    )
+
+
 def solution(mesh):
+    def chosen(*arrays):
+        heads = arrays[3].shape[1] // HEAD
+        return (on_split_device if heads % 2 == 0 else on_device)(*arrays)
+
     return jax.shard_map(
-        on_device,
+        chosen,
         mesh=mesh,
         in_specs=(
             P("dp", "tensor"),

time: 239 us -> 242 us (1.013)
  Pallas kernels: 226 us -> 231 us
    pallas_call x1, Pallas kernels: 226 us -> 231 us  [on_split_device(): pl.pallas_call(functools.partial(split_kernel, n, nt), out_shape=(jax.Sha...]
where the time goes in v5:
time: 242 us; the launch traced here: 240 us
  Pallas kernels  231 us (95%)
  local copies, waits for them, and re-layouts  7.81 us (3%)
    pallas_call x1, Pallas kernels, on_split_device(): pl.pallas_call(functools.partial(split_kernel, n, nt), out_shape=(jax.Sha...  231 us
    unnamed x21, local copies, waits for them, and re-layouts  7.2 us

profile of v5, /device:TPU:26, one launch (start us, length us, event | category | flops | bytes accessed | tf_op | source)
XLA Modules:
  0.0 240.0 jit_solution(13441793925626735403)
XLA Ops:
  0.6 0.0 copy-start.2
  0.7 0.1 pad_maximum_fusion
  0.7 0.6 broadcast_in_dim.13.freq
  1.3 0.0 copy-done.2
  1.3 0.0 copy-start.3
  1.3 0.6 broadcast_in_dim.14
  1.9 0.1 copy-done.3
  2.0 0.0 copy-start.4
  2.0 0.7 copy.13.seq_length
  2.7 0.0 copy-done.4
  2.7 0.0 copy-start.5
  2.7 0.7 copy.14.home_offset
  3.4 0.0 copy-done.5
  3.4 0.0 copy-start.6
  3.4 0.7 copy.15.dest_shard
  4.1 0.0 copy-done.6
  4.1 0.7 copy.16.dest_offset
  4.8 230.9 %shard_map.121 = (bf16[256,2048]{1,0:T(8,128)(2,1)}, bf16[128,2048]{1,0:T(8,128)(2,1)}, f32[256,512]{1,0:T(8,128)}) custom-call(s32[16,4]{1,0:T(8,128)} %copy.13.seq_length, s32[16,4]{1,0:T(8,128)} %copy.14.home_offset, s32[16,4]{1,0:T(8,128)} %copy.15.dest_shard, s32[16,4]{1,0:T(8,128)} %copy.16.dest_offset, bf16[128,2048]{1,0:T(8,128)(2,1)} %hidden.1, ...), custom_call_target="tpu_custom_call" | custom-call | flops 8000000000 | bytes 8000000 | tf_op jit(solution)/shard_map/pallas_call | solution.py:1487
  235.6 0.0 copy-start.1
  235.6 2.4 copy.20
  238.0 0.0 copy-done.1
  238.0 0.0 copy-start
  238.0 0.8 copy.21
  238.8 0.4 copy-done
  239.2 0.8 copy.22
  (1 shorter events, 0.0 us)
Async XLA Ops:
  0.6 0.7 copy-start.2
  1.3 0.7 copy-start.3
  2.0 0.7 copy-start.4
  2.7 0.7 copy-start.5
  3.4 0.7 copy-start.6
  235.6 2.4 copy-start.1
  238.0 1.2 copy-start

commit v6 on v5

--- a/solution.py
+++ b/solution.py
@@ -814,8 +814,8 @@
         copy.start()
 
     def w_view(h, zz, xx, which):
-        rows = pl.multiple_of((4 * zz + 2 * which) * blk, 2 * blk)
-        return wbuf.at[h, pl.ds(rows, 2 * blk)]
+        rows = pl.multiple_of((4 * zz + 2 * which + lax.rem(h, 2)) * blk, blk)
+        return wbuf.at[lax.div(h, 2), pl.ds(rows, blk)]
 
     def g_view(h, zz, xx, which):
         rows = pl.multiple_of((4 * zz + 2 * which) * TOK_DEV, 2 * TOK_DEV)
@@ -935,12 +935,17 @@
     w_sems = (wzs, wzr, None, None, wss, wsr)
     g_sems = (gzs, gzr, gxs, gxr, gss, gsr)
     early = zs // 2
+    def w_step(h, k):
+        step(w_view, w_sems, 2 * h, k)
+        step(w_view, w_sems, 2 * h + 1, k)
+
     def begin_weights(h):
         for load in loads_of(h):
             load.wait()
         for swap in swaps_of(h, other_spot):
             swap.wait_recv()
-        begin(w_view, w_sems, h)
+        begin(w_view, w_sems, 2 * h)
+        begin(w_view, w_sems, 2 * h + 1)
 
     begin_weights(0)
 
@@ -1009,7 +1014,7 @@
     for h in range(1, hh):
         begin_weights(h)
     for k in range(1, early):
-        step(w_view, w_sems, 0, k)
+        w_step(0, k)
 
     for copy in tensor_copies:
         copy.wait_send()
@@ -1068,7 +1073,7 @@
         for j in range(1, nt):
             share_copy(j, t).start()
 
-    step(w_view, w_sems, 0, early)
+    w_step(0, early)
 
     row = lax.broadcasted_iota(jnp.int32, (TOK_DEV, TOK_DEV), 0)
     col = lax.broadcasted_iota(jnp.int32, (TOK_DEV, TOK_DEV), 1)
@@ -1210,18 +1215,14 @@
 
             @pl.when(h < hh)
             def _():
-                step(w_view, w_sems, h, early + k)
-
-            @pl.when((h >= 2) & (h < hh))
-            def _():
-                step(g_view, g_sems, h - 2, 2 * k - 1)
-                step(g_view, g_sems, h - 2, 2 * k)
+                w_step(h, early + k)
 
             if k == 1:
 
                 @pl.when(h >= 1)
                 def _():
-                    gathered(w_view, w_sems, h - 1)
+                    gathered(w_view, w_sems, 2 * h - 2)
+                    gathered(w_view, w_sems, 2 * h - 1)
                     acc[...] = jnp.zeros_like(acc)
                     project_head(h - 1, 0, n // 2)
 
@@ -1231,9 +1232,14 @@
                 def _():
                     attend_head(h - 1)
 
+            @pl.when(h >= 2)
+            def _():
+                step(g_view, g_sems, h - 2, 2 * k - 1)
+                step(g_view, g_sems, h - 2, 2 * k)
+
             @pl.when(h + 1 < hh)
             def _():
-                step(w_view, w_sems, h + 1, k)
+                w_step(h + 1, k)
 
             if k == 1:
 
@@ -1259,7 +1265,7 @@
 
     lax.fori_loop(0, hh + 1, round_of, 0)
 
-    last = range(max(hh - 2, 0), hh)
+    last = range(hh - 1, hh)
     for j in range(n):
         pxs[j] = pacc[j, :, TOK_DEV:].astype(BF16)
     half_swap = remote(pxs, pxr, qsend.at[2], qrecv.at[2], {"dp": across})
@@ -1338,7 +1344,8 @@
     gvw_ref[...] = gvw_acc[...]
 
     def finish(h, carry):
-        drained(w_view, w_sems, h)
+        drained(w_view, w_sems, 2 * h)
+        drained(w_view, w_sems, 2 * h + 1)
         drained(g_view, g_sems, h)
         return carry
 

time: 242 us -> 237 us (0.979)
  Pallas kernels: 231 us -> 227 us
    pallas_call x1, Pallas kernels: 231 us -> 227 us  [on_split_device(): pl.pallas_call(functools.partial(split_kernel, n, nt), out_shape=(jax.Sha...]
where the time goes in v6:
time: 237 us; the launch traced here: 236 us
  Pallas kernels  227 us (96%)
  local copies, waits for them, and re-layouts  7.81 us (3%)
    pallas_call x1, Pallas kernels, on_split_device(): pl.pallas_call(functools.partial(split_kernel, n, nt), out_shape=(jax.Sha...  227 us
    unnamed x21, local copies, waits for them, and re-layouts  7.2 us

profile of v6, /device:TPU:26, one launch (start us, length us, event | category | flops | bytes accessed | tf_op | source)
XLA Modules:
  0.0 236.2 jit_solution(3393170633012336455)
XLA Ops:
  0.6 0.0 copy-start.2
  0.7 0.1 pad_maximum_fusion
  0.7 0.6 broadcast_in_dim.13.freq
  1.3 0.0 copy-done.2
  1.3 0.0 copy-start.3
  1.3 0.6 broadcast_in_dim.14
  1.9 0.1 copy-done.3
  2.0 0.0 copy-start.4
  2.0 0.7 copy.13.seq_length
  2.7 0.0 copy-done.4
  2.7 0.0 copy-start.5
  2.7 0.7 copy.14.home_offset
  3.4 0.0 copy-done.5
  3.4 0.0 copy-start.6
  3.4 0.7 copy.15.dest_shard
  4.1 0.0 copy-done.6
  4.1 0.7 copy.16.dest_offset
  4.8 227.0 %shard_map.121 = (bf16[256,2048]{1,0:T(8,128)(2,1)}, bf16[128,2048]{1,0:T(8,128)(2,1)}, f32[256,512]{1,0:T(8,128)}) custom-call(s32[16,4]{1,0:T(8,128)} %copy.13.seq_length, s32[16,4]{1,0:T(8,128)} %copy.14.home_offset, s32[16,4]{1,0:T(8,128)} %copy.15.dest_shard, s32[16,4]{1,0:T(8,128)} %copy.16.dest_offset, bf16[128,2048]{1,0:T(8,128)(2,1)} %hidden.1, ...), custom_call_target="tpu_custom_call" | custom-call | flops 8000000000 | bytes 8000000 | tf_op jit(solution)/shard_map/pallas_call | solution.py:1494
  231.8 0.0 copy-start.1
  231.8 2.4 copy.20
  234.2 0.0 copy-done.1
  234.2 0.0 copy-start
  234.2 0.8 copy.21
  235.0 0.4 copy-done
  235.4 0.8 copy.22
  (1 shorter events, 0.0 us)
Async XLA Ops:
  0.6 0.7 copy-start.2
  1.3 0.7 copy-start.3
  2.0 0.7 copy-start.4
  2.7 0.7 copy-start.5
  3.4 0.7 copy-start.6
  231.8 2.4 %copy-start.1 = (bf16[128,2048]{1,0:T(8,128)(2,1)S(1)}, bf16[128,2048]{1,0:T(8,128)(2,1)}, u32[]{:S(2)}) copy-start(bf16[128,2048]{1,0:T(8,128)(2,1)} %get-tuple-element.7) | copy-start | bytes 1572868
  234.2 1.2 copy-start

commit v7 on v6

--- a/solution.py
+++ b/solution.py
@@ -1266,15 +1266,27 @@
     lax.fori_loop(0, hh + 1, round_of, 0)
 
     last = range(hh - 1, hh)
+    half_swaps = []
     for j in range(n):
         pxs[j] = pacc[j, :, TOK_DEV:].astype(BF16)
-    half_swap = remote(pxs, pxr, qsend.at[2], qrecv.at[2], {"dp": across})
-    half_swap.start()
+        if j % 4 == 3:
+            piece = pl.ds(j - 3, 4)
+            half_swaps.append(
+                remote(
+                    pxs.at[piece],
+                    pxr.at[piece],
+                    qsend.at[2 + j // 4],
+                    qrecv.at[2 + j // 4],
+                    {"dp": across},
+                )
+            )
+            half_swaps[-1].start()
     from_other(hh - 1)
     for h in last:
         step(g_view, g_sems, h, 1)
-    half_swap.wait()
     for j in range(n):
+        if j % 4 == 0:
+            half_swaps[j // 4].wait()
         total = pacc[j, :, :TOK_DEV] + pxr[j].astype(F32)
         shard = j - j % 4 + 2 * (j % 2) + (j % 4) // 2
         first = shard * blk % TILE
@@ -1545,8 +1557,8 @@
             dma((nt,)),
             dma((hh,)),
             dma((hh,)),
-            dma((3,)),
-            dma((3,)),
+            dma((2 + n // 4,)),
+            dma((2 + n // 4,)),
             dma((nt, 2)),
             dma((nt, 2)),
             dma((n,)),

time: 237 us -> 236 us (level)
  no operation moved by 1% of the time
where the time goes in v7:
time: 236 us
  Pallas kernels  227 us (96%)
  local copies, waits for them, and re-layouts  7.81 us (3%)
    pallas_call x1, Pallas kernels, on_split_device(): pl.pallas_call(functools.partial(split_kernel, n, nt), out_shape=(jax.Sha...  227 us
    unnamed x21, local copies, waits for them, and re-layouts  7.2 us

profile of v7, /device:TPU:26, one launch (start us, length us, event | category | flops | bytes accessed | tf_op | source)
XLA Modules:
  0.0 236.1 jit_solution(8067909558497377246)
XLA Ops:
  0.6 0.0 copy-start.2
  0.7 0.1 pad_maximum_fusion
  0.7 0.6 broadcast_in_dim.13.freq
  1.3 0.0 copy-done.2
  1.3 0.0 copy-start.3
  1.3 0.6 broadcast_in_dim.14
  1.9 0.1 copy-done.3
  2.0 0.0 copy-start.4
  2.0 0.7 copy.13.seq_length
  2.7 0.0 copy-done.4
  2.7 0.0 copy-start.5
  2.7 0.7 copy.14.home_offset
  3.4 0.0 copy-done.5
  3.4 0.0 copy-start.6
  3.4 0.7 copy.15.dest_shard
  4.1 0.0 copy-done.6
  4.1 0.7 copy.16.dest_offset
  4.8 227.0 %shard_map.121 = (bf16[256,2048]{1,0:T(8,128)(2,1)}, bf16[128,2048]{1,0:T(8,128)(2,1)}, f32[256,512]{1,0:T(8,128)}) custom-call(s32[16,4]{1,0:T(8,128)} %copy.13.seq_length, s32[16,4]{1,0:T(8,128)} %copy.14.home_offset, s32[16,4]{1,0:T(8,128)} %copy.15.dest_shard, s32[16,4]{1,0:T(8,128)} %copy.16.dest_offset, bf16[128,2048]{1,0:T(8,128)(2,1)} %hidden.1, ...), custom_call_target="tpu_custom_call" | custom-call | flops 8000000000 | bytes 8000000 | tf_op jit(solution)/shard_map/pallas_call | solution.py:1506
  231.7 0.0 copy-start.1
  231.7 2.4 %copy.20 = bf16[256,2048]{1,0:T(8,128)(2,1)} copy(bf16[256,2048]{1,0:T(8,128)(2,1)} %get-tuple-element.6) | data formatting | bytes 2097152
  234.1 0.0 copy-done.1
  234.1 0.0 copy-start
  234.1 0.8 copy.21
  234.9 0.4 copy-done
  235.3 0.8 copy.22
  (1 shorter events, 0.0 us)
Async XLA Ops:
  0.6 0.7 copy-start.2
  1.3 0.7 copy-start.3
  2.0 0.7 copy-start.4
  2.7 0.7 copy-start.5
  3.4 0.7 copy-start.6
  231.7 2.4 %copy-start.1 = (bf16[128,2048]{1,0:T(8,128)(2,1)S(1)}, bf16[128,2048]{1,0:T(8,128)(2,1)}, u32[]{:S(2)}) copy-start(bf16[128,2048]{1,0:T(8,128)(2,1)} %get-tuple-element.7) | copy-start | bytes 1572868
  234.1 1.2 copy-start
